TPU v7x, 32 devices: a whole 2x2x4 slice. The times are simulated.
32 devices in a mesh: dp: 4 (over y, x), fsdp: 8 (over z, core).
Axes of the slice: x: 2, y: 2, z: 4, core: 2. Of those that a mesh axis runs over, the one named last changes fastest.
Arguments:
- tokens: bfloat16 [32768, 768], P(('dp', 'fsdp')), may hold values from -12 to 12
- cotangent: bfloat16 [32768, 768], P(('dp', 'fsdp')), may hold values from -6 to 6
- lengths: int32 [32, 16], P(('dp', 'fsdp')), may hold values from 1 to 781, 1024 in all within a row
- qkv_weight: float32 [3, 768, 768], P(None, ('dp', 'fsdp')), may hold values from -0.109375 to 0.109375
- out_weight: float32 [768, 768], P(('dp', 'fsdp')), may hold values from -0.4375 to 0.4375
- in_weight: float32 [768, 3072], P(('dp', 'fsdp')), may hold values from -0.25980762 to 0.25980762
- down_weight: float32 [3072, 768], P(('dp', 'fsdp')), may hold values from -0.109375 to 0.109375
- vectors: float32 [12, 768], P(None, ('dp', 'fsdp')), may hold values from -1 to 2.5
- qkv_first: float32 [3, 768, 768], P(None, ('dp', 'fsdp')), may hold values from -8.59375e-05 to 8.59375e-05
- out_first: float32 [768, 768], P(('dp', 'fsdp')), may hold values from -3.3854165e-05 to 3.3854165e-05
- in_first: float32 [768, 3072], P(('dp', 'fsdp')), may hold values from -0.00011458333 to 0.00011458333
- down_first: float32 [3072, 768], P(('dp', 'fsdp')), may hold values from -0.00028645832 to 0.00028645832
- vec_first: float32 [12, 768], P(None, ('dp', 'fsdp')), may hold values from -0.00013020834 to 0.00013020834
- qkv_second: float32 [3, 768, 768], P(None, ('dp', 'fsdp')), may hold values from 9.536743e-12 to 3.814697e-11
- out_second: float32 [768, 768], P(('dp', 'fsdp')), may hold values from 1.5258789e-12 to 6.1035157e-12
- in_second: float32 [768, 3072], P(('dp', 'fsdp')), may hold values from 1.695421e-11 to 6.781684e-11
- down_second: float32 [3072, 768], P(('dp', 'fsdp')), may hold values from 1.05963814e-10 to 4.2385526e-10
- vec_second: float32 [12, 768], P(None, ('dp', 'fsdp')), may hold values from 2.6490954e-11 to 1.05963814e-10
Outputs:
- layer_out: bfloat16 [32768, 768], P(('dp', 'fsdp'))
- input_grad: bfloat16 [32768, 768], P(('dp', 'fsdp'))
- grad_norm: float32 [], replicated
- qkv_new: float32 [3, 768, 768], P(None, ('dp', 'fsdp'))
- out_new: float32 [768, 768], P(('dp', 'fsdp'))
- in_new: float32 [768, 3072], P(('dp', 'fsdp'))
- down_new: float32 [3072, 768], P(('dp', 'fsdp'))
- vectors_new: float32 [12, 768], P(None, ('dp', 'fsdp'))
- qkv_first_new: float32 [3, 768, 768], P(None, ('dp', 'fsdp'))
- out_first_new: float32 [768, 768], P(('dp', 'fsdp'))
- in_first_new: float32 [768, 3072], P(('dp', 'fsdp'))
- down_first_new: float32 [3072, 768], P(('dp', 'fsdp'))
- vec_first_new: float32 [12, 768], P(None, ('dp', 'fsdp'))
- qkv_second_new: float32 [3, 768, 768], P(None, ('dp', 'fsdp'))
- out_second_new: float32 [768, 768], P(('dp', 'fsdp'))
- in_second_new: float32 [768, 3072], P(('dp', 'fsdp'))
- down_second_new: float32 [3072, 768], P(('dp', 'fsdp'))
- vec_second_new: float32 [12, 768], P(None, ('dp', 'fsdp'))
Inputs may be any that keep to these rules, and one draw needn't show every extreme that they name: Each device's 16 lengths sum to 1024; its longest is 781.
All inputs are finite; a program needn't handle non-finite values.
Results may differ from a plain program's by a relative error of at most 0.015.
The roundings to bfloat16 on the way count: a program that leaves them out, or rounds other values in their place, can miss the bound.
Values may be sent and summed in bfloat16 or wider, within the bound.
A program may use at most 256 MiB of HBM per device.

v0:
```python
import jax
import jax.numpy as jnp
from jax import lax
from jax.sharding import PartitionSpec as P

D = 768
H = 12
HD = 64
FF = 3072
TOK_DEV = 1024
STEP = 10


moment_decay = 0.9
square_decay = 0.999
learn_rate = 0.02
vector_rate = 0.15
weight_decay = 0.01
adam_epsilon = 1e-08
clip_limit = 1.0
norm_epsilon = 1e-05


def layer_norm(hidden, gain_vec, shift_vec):
    center = hidden - jnp.mean(hidden, axis=-1, keepdims=True)
    spread = jnp.mean(center * center, axis=-1, keepdims=True)
    return center * lax.rsqrt(spread + norm_epsilon) * gain_vec + shift_vec


def gelu_exact(values):
    return jax.nn.gelu(values, approximate=False)


def segment_ids(lengths):
    bounds = jnp.cumsum(lengths, axis=-1)
    places = jnp.arange(TOK_DEV, dtype=jnp.int32)
    return jnp.sum((places[None, :, None] >= bounds[:, None, :]).astype(jnp.int32), axis=-1)


def inner_dot(left, right):
    return lax.dot_general(
        left, right, (((0,), (0,)), ((), ())), preferred_element_type=jnp.float32
    )


def outer_dot(left, right):
    return lax.dot_general(
        left, right, (((1,), (1,)), ((), ())), preferred_element_type=jnp.float32
    )


def masked_scores(query_block, key_heads, segment_block, segment):
    scores = jnp.einsum(
        "qhd,khd->hqk", query_block, key_heads, preferred_element_type=jnp.float32
    ) * HD ** (-0.5)
    allowed = segment_block[:, None] == segment[None, :]
    return jnp.where(allowed[None], scores, -1e30)


def attend_forward(query_heads, key_heads, value_heads, segment, block_rows):
    blocks_count = query_heads.shape[0] // block_rows

    def one_block(block_index):
        row_start = block_index * block_rows
        query_block = lax.dynamic_slice_in_dim(query_heads, row_start, block_rows, 0)
        segment_block = lax.dynamic_slice_in_dim(segment, row_start, block_rows, 0)
        scores = masked_scores(query_block, key_heads, segment_block, segment)
        largest = jnp.max(scores, axis=-1, keepdims=True)
        exponent = jnp.exp(scores - largest)
        totals = jnp.sum(exponent, axis=-1, keepdims=True)
        weights = (exponent / totals).astype(jnp.bfloat16)
        context = jnp.einsum(
            "hqk,khd->qhd", weights, value_heads, preferred_element_type=jnp.float32
        )
        return (context, (largest + jnp.log(totals))[..., 0])

    contexts, logsums = lax.map(one_block, jnp.arange(blocks_count, dtype=jnp.int32))
    return (contexts.reshape(query_heads.shape), logsums)


def attend_backward(query_heads, key_heads, value_heads, segment, logsums, grad_heads, block_rows):
    blocks_count = query_heads.shape[0] // block_rows

    def one_block(carry, block_index):
        key_grad, value_grad = carry
        row_start = block_index * block_rows
        query_block = lax.dynamic_slice_in_dim(query_heads, row_start, block_rows, 0)
        segment_block = lax.dynamic_slice_in_dim(segment, row_start, block_rows, 0)
        grad_block = lax.dynamic_slice_in_dim(grad_heads, row_start, block_rows, 0)
        scores = masked_scores(query_block, key_heads, segment_block, segment)
        weights = jnp.exp(scores - logsums[block_index][..., None])
        grad_weights = jnp.einsum(
            "qhd,khd->hqk", grad_block, value_heads, preferred_element_type=jnp.float32
        )
        grad_scores = weights * (
            grad_weights - jnp.sum(weights * grad_weights, axis=-1, keepdims=True)
        )
        score_low = grad_scores.astype(jnp.bfloat16)
        query_grad = jnp.einsum(
            "hqk,khd->qhd", score_low, key_heads, preferred_element_type=jnp.float32
        ) * HD ** (-0.5)
        key_grad = key_grad + jnp.einsum(
            "hqk,qhd->khd", score_low, query_block, preferred_element_type=jnp.float32
        ) * HD ** (-0.5)
        value_grad = value_grad + jnp.einsum(
            "hqk,qhd->khd",
            weights.astype(jnp.bfloat16),
            grad_block,
            preferred_element_type=jnp.float32,
        )
        return ((key_grad, value_grad), query_grad)

    zeros_heads = jnp.zeros(query_heads.shape, jnp.float32)
    (key_grad, value_grad), query_grads = lax.scan(
        one_block, (zeros_heads, zeros_heads), jnp.arange(blocks_count, dtype=jnp.int32)
    )
    return (query_grads.reshape(query_heads.shape), key_grad, value_grad)


def adam_step(weight, gradient, first_old, second_old, decay_rate, step_rate):
    first_new = moment_decay * first_old + (1.0 - moment_decay) * gradient
    second_new = square_decay * second_old + (1.0 - square_decay) * gradient * gradient
    first_hat = first_new / (1.0 - moment_decay**STEP)
    second_hat = second_new / (1.0 - square_decay**STEP)
    weight_new = weight - step_rate * (
        first_hat / (jnp.sqrt(second_hat) + adam_epsilon) + decay_rate * weight
    )
    return (weight_new, first_new, second_new)


def per_device(
    tokens,
    cotangent,
    lengths,
    qkv_weight,
    out_weight,
    in_weight,
    down_weight,
    vectors,
    qkv_first,
    out_first,
    in_first,
    down_first,
    vec_first,
    qkv_second,
    out_second,
    in_second,
    down_second,
    vec_second,
):
    qkv_full, out_full, in_full, down_full, vec_full = (
        lax.all_gather(qkv_weight.astype(jnp.bfloat16), ("dp", "fsdp"), axis=1, tiled=True),
        lax.all_gather(out_weight.astype(jnp.bfloat16), ("dp", "fsdp"), axis=0, tiled=True),
        lax.all_gather(in_weight.astype(jnp.bfloat16), ("dp", "fsdp"), axis=0, tiled=True),
        lax.all_gather(down_weight.astype(jnp.bfloat16), ("dp", "fsdp"), axis=0, tiled=True),
        lax.all_gather(vectors.astype(jnp.bfloat16), ("dp", "fsdp"), axis=1, tiled=True),
    )
    vec_float = vec_full.astype(jnp.float32)
    token_rows = tokens.shape[0]
    block_rows = min(512, token_rows)
    segment = segment_ids(lengths)[0]
    queries = (
        jnp.dot(tokens, qkv_full[0], preferred_element_type=jnp.float32) + vec_float[0]
    ).astype(jnp.bfloat16)
    keys_low = jnp.dot(tokens, qkv_full[1], preferred_element_type=jnp.float32).astype(jnp.bfloat16)
    values_low = (
        jnp.dot(tokens, qkv_full[2], preferred_element_type=jnp.float32) + vec_float[1]
    ).astype(jnp.bfloat16)
    query_heads = queries.reshape(token_rows, H, HD)
    key_heads = keys_low.reshape(token_rows, H, HD)
    value_heads = values_low.reshape(token_rows, H, HD)
    contexts, logsums = attend_forward(query_heads, key_heads, value_heads, segment, block_rows)
    context_low = contexts.reshape(token_rows, D).astype(jnp.bfloat16)
    branch = jnp.dot(context_low, out_full, preferred_element_type=jnp.float32) + vec_float[2]
    normed, norm_one_back = jax.vjp(
        layer_norm, tokens.astype(jnp.float32) + branch, vec_float[4], vec_float[5]
    )
    normed_low = normed.astype(jnp.bfloat16)
    hidden_pre = jnp.dot(normed_low, in_full, preferred_element_type=jnp.float32) + vec_float[
        8:12
    ].reshape(FF)
    hidden, gelu_back = jax.vjp(gelu_exact, hidden_pre)
    hidden_low = hidden.astype(jnp.bfloat16)
    ffn_out = jnp.dot(hidden_low, down_full, preferred_element_type=jnp.float32) + vec_float[3]
    result, norm_two_back = jax.vjp(layer_norm, normed + ffn_out, vec_float[6], vec_float[7])
    qkv_back, out_back, in_back, down_back = (
        lax.all_gather(qkv_weight.astype(jnp.bfloat16), ("dp", "fsdp"), axis=1, tiled=True),
        lax.all_gather(out_weight.astype(jnp.bfloat16), ("dp", "fsdp"), axis=0, tiled=True),
        lax.all_gather(in_weight.astype(jnp.bfloat16), ("dp", "fsdp"), axis=0, tiled=True),
        lax.all_gather(down_weight.astype(jnp.bfloat16), ("dp", "fsdp"), axis=0, tiled=True),
    )
    grad_second_in, grad_gain_two, grad_shift_two = norm_two_back(cotangent.astype(jnp.float32))
    grad_ffn = grad_second_in.astype(jnp.bfloat16)
    grad_bias_down = jnp.sum(grad_ffn.astype(jnp.float32), axis=0)
    grad_down = inner_dot(hidden_low, grad_ffn)
    grad_hidden = outer_dot(grad_ffn, down_back)
    grad_pre = gelu_back(grad_hidden)[0].astype(jnp.bfloat16)
    grad_bias_hidden = jnp.sum(grad_pre.astype(jnp.float32), axis=0)
    grad_in = inner_dot(normed_low, grad_pre)
    grad_normed = grad_second_in + outer_dot(grad_pre, in_back)
    grad_first_in, grad_gain_one, grad_shift_one = norm_one_back(grad_normed)
    grad_branch = grad_first_in.astype(jnp.bfloat16)
    grad_bias_out = jnp.sum(grad_branch.astype(jnp.float32), axis=0)
    grad_out = inner_dot(context_low, grad_branch)
    grad_context = outer_dot(grad_branch, out_back).astype(jnp.bfloat16)
    query_grad, key_grad, value_grad = attend_backward(
        query_heads,
        key_heads,
        value_heads,
        segment,
        logsums,
        grad_context.reshape(token_rows, H, HD),
        block_rows,
    )
    query_grad_low = query_grad.reshape(token_rows, D).astype(jnp.bfloat16)
    key_grad_low = key_grad.reshape(token_rows, D).astype(jnp.bfloat16)
    value_grad_low = value_grad.reshape(token_rows, D).astype(jnp.bfloat16)
    grad_qkv = jnp.stack(
        [
            inner_dot(tokens, query_grad_low),
            inner_dot(tokens, key_grad_low),
            inner_dot(tokens, value_grad_low),
        ]
    )
    grad_tokens = (
        grad_first_in
        + outer_dot(query_grad_low, qkv_back[0])
        + outer_dot(key_grad_low, qkv_back[1])
        + outer_dot(value_grad_low, qkv_back[2])
    )
    grad_rows = jnp.stack(
        [
            jnp.sum(query_grad_low.astype(jnp.float32), axis=0),
            jnp.sum(value_grad_low.astype(jnp.float32), axis=0),
            grad_bias_out,
            grad_bias_down,
            grad_gain_one,
            grad_shift_one,
            grad_gain_two,
            grad_shift_two,
        ]
    )
    grad_vec = jnp.concatenate([grad_rows, grad_bias_hidden.reshape(4, D)], axis=0)
    qkv_shard, out_shard, in_shard, down_shard, vec_shard = (
        lax.psum_scatter(grad_qkv, ("dp", "fsdp"), scatter_dimension=1, tiled=True),
        lax.psum_scatter(grad_out, ("dp", "fsdp"), scatter_dimension=0, tiled=True),
        lax.psum_scatter(grad_in, ("dp", "fsdp"), scatter_dimension=0, tiled=True),
        lax.psum_scatter(grad_down, ("dp", "fsdp"), scatter_dimension=0, tiled=True),
        lax.psum_scatter(grad_vec, ("dp", "fsdp"), scatter_dimension=1, tiled=True),
    )
    local_squares = (
        jnp.sum(qkv_shard * qkv_shard)
        + jnp.sum(out_shard * out_shard)
        + jnp.sum(in_shard * in_shard)
        + jnp.sum(down_shard * down_shard)
        + jnp.sum(vec_shard * vec_shard)
    )
    total_sum = lax.psum(local_squares, ("dp", "fsdp"))
    grad_norm = jnp.sqrt(total_sum)
    factor = jnp.minimum(1.0, clip_limit / (grad_norm + 1e-06))
    qkv_new, qkv_first_new, qkv_second_new = adam_step(
        qkv_weight, factor * qkv_shard, qkv_first, qkv_second, weight_decay, learn_rate
    )
    out_new, out_first_new, out_second_new = adam_step(
        out_weight, factor * out_shard, out_first, out_second, weight_decay, learn_rate
    )
    in_new, in_first_new, in_second_new = adam_step(
        in_weight, factor * in_shard, in_first, in_second, weight_decay, learn_rate
    )
    down_new, down_first_new, down_second_new = adam_step(
        down_weight, factor * down_shard, down_first, down_second, weight_decay, learn_rate
    )
    vectors_new, vec_first_new, vec_second_new = adam_step(
        vectors, factor * vec_shard, vec_first, vec_second, 0.0, vector_rate
    )
    return (
        result.astype(jnp.bfloat16),
        grad_tokens.astype(jnp.bfloat16),
        grad_norm,
        qkv_new,
        out_new,
        in_new,
        down_new,
        vectors_new,
        qkv_first_new,
        out_first_new,
        in_first_new,
        down_first_new,
        vec_first_new,
        qkv_second_new,
        out_second_new,
        in_second_new,
        down_second_new,
        vec_second_new,
    )


def solution(mesh):
    in_specs = (
        P(("dp", "fsdp"), None),
        P(("dp", "fsdp"), None),
        P(("dp", "fsdp"), None),
        P(None, ("dp", "fsdp"), None),
        P(("dp", "fsdp"), None),
        P(("dp", "fsdp"), None),
        P(("dp", "fsdp"), None),
        P(None, ("dp", "fsdp")),
        P(None, ("dp", "fsdp"), None),
        P(("dp", "fsdp"), None),
        P(("dp", "fsdp"), None),
        P(("dp", "fsdp"), None),
        P(None, ("dp", "fsdp")),
        P(None, ("dp", "fsdp"), None),
        P(("dp", "fsdp"), None),
        P(("dp", "fsdp"), None),
        P(("dp", "fsdp"), None),
        P(None, ("dp", "fsdp")),
    )
    out_specs = (
        P(("dp", "fsdp"), None),
        P(("dp", "fsdp"), None),
        P(),
        P(None, ("dp", "fsdp"), None),
        P(("dp", "fsdp"), None),
        P(("dp", "fsdp"), None),
        P(("dp", "fsdp"), None),
        P(None, ("dp", "fsdp")),
        P(None, ("dp", "fsdp"), None),
        P(("dp", "fsdp"), None),
        P(("dp", "fsdp"), None),
        P(("dp", "fsdp"), None),
        P(None, ("dp", "fsdp")),
        P(None, ("dp", "fsdp"), None),
        P(("dp", "fsdp"), None),
        P(("dp", "fsdp"), None),
        P(("dp", "fsdp"), None),
        P(None, ("dp", "fsdp")),
    )
    return jax.shard_map(
        per_device, mesh=mesh, in_specs=in_specs, out_specs=out_specs, check_vma=False
    )
```

profile of v0, /device:TPU:0, one launch (start us, length us, event | category | flops | bytes accessed | tf_op | source)
XLA Modules:
  0.0 1071.1 jit_solution(10240012939565862663)
XLA Ops:
  14.8 44.0 %all-gather = bf16[32,24,12]{1,2,0:T(8,128)(2,1)S(1)} all-gather(bf16[1,24,12]{1,2,0:T(8,128)(2,1)S(1)} %convert_bitcast_fusion), channel_id=1, replica_groups=mesh['dp'=4,'fsdp'=8] {'dp','fsdp'}, dimensions={0}, use_global_device_ids=true | all-gather | bytes 19008 | tf_op jit(solution)/shard_map/all_gather | solution.py:156
  64.7 10.2 all-gather.6.cloned.1.call-done
  74.9 2.9 convolution_convert_fusion.1
  77.8 2.7 add_convert_fusion.3
  83.3 72.9 %while.27 = (s32[]{:T(128)}, bf16[2,512,12,64]{1,3,2,0:T(8,128)(2,1)}, f32[2,12,512]{2,1,0:T(8,128)S(1)}, s32[2]{0:T(128)S(1)}, s32[1024]{0:T(1024)S(1)}, /*inde...) while((s32[]{:T(128)}, ...), condition=%wide.region_5.6_spmd, body=%wide.region_2.5_spmd.sunk | while | flops 1686628352 | bytes 190286064 | solution.py:77
  85.0 10.6 fusion.113
  95.6 12.3 %fusion.114 = f32[12,512]{1,0:T(8,128)S(1)} fusion(f32[12,512,1024]{2,1,0:T(8,128)} %get-tuple-element.484, f32[12,512]{1,0:T(8,128)S(1)} %get-tuple-element.485, pred[512,1024]{1,0:T(8,128)(4,1)S(1)} %broadcast_compare_fusion.4), kind=kLoop, calls=%fused_computation.4.clone.1 | loop fusion | flops 25159680 | bytes 25739264 | tf_op jit(solution)/shard_map/while/body/eval_jaxpr/reduce_sum | solution.py:70
  107.9 3.1 copy-done
  111.0 8.5 bitcast_dynamic-update-slice_fusion.6
  121.2 10.7 fusion.113
  131.9 12.4 %fusion.114 = f32[12,512]{1,0:T(8,128)S(1)} fusion(f32[12,512,1024]{2,1,0:T(8,128)} %get-tuple-element.484, f32[12,512]{1,0:T(8,128)S(1)} %get-tuple-element.485, pred[512,1024]{1,0:T(8,128)(4,1)S(1)} %broadcast_compare_fusion.4), kind=kLoop, calls=%fused_computation.4.clone.1 | loop fusion | flops 25159680 | bytes 25739264 | tf_op jit(solution)/shard_map/while/body/eval_jaxpr/reduce_sum | solution.py:70
  144.3 3.2 copy-done
  147.4 8.5 bitcast_dynamic-update-slice_fusion.6
  156.2 4.2 copy.110
  162.0 3.8 fusion.58
  166.3 31.5 %all-gather.10.cloned.1.call-done = bf16[768,3072]{1,0:T(8,128)(2,1)} async-done(((bf16[24,3072]{1,0:T(8,128)(2,1)}), bf16[768,3072]{1,0:T(8,128)(2,1)}) %all-gather.10.cloned.1.call-update) | async-done | bytes 4718608 | tf_op jit(solution)/shard_map/all_gather | solution.py:154
  197.8 37.6 %multiply_convert_fusion.1 = (bf16[1024,3072]{1,0:T(8,128)(2,1)}, f32[1024,3072]{1,0:T(8,128)}, f32[1024,3072]{1,0:T(8,128)}) fusion(f32[3072]{0:T(1024)S(1)} %copy-done.54, bf16[768,3072]{1,0:T(8,128)(2,1)} %all-gather.10.cloned.1.call-done, f32[1024,768]{0,1:T(8,128)S(1)} %get-tuple-element.357, f32[768]{0:T(1024)S(1)} %copy-done.56, ...), kind=kOutput, calls=%fused_computation.41 | convolution fusion | flops 5043388416 | bytes 39348224 | tf_op jit(solution)/shard_map/dot_general | solution.py:179
  235.4 28.3 %all-gather.12.cloned.1.call-done = bf16[3072,768]{1,0:T(8,128)(2,1)} async-done(((bf16[96,768]{1,0:T(8,128)(2,1)}), bf16[3072,768]{1,0:T(8,128)(2,1)}) %all-gather.12.cloned.1.call-update) | async-done | bytes 4718608 | tf_op jit(solution)/shard_map/all_gather | solution.py:155
  263.7 21.6 %fusion.59 = (f32[1024]{0:T(1024)S(1)}, f32[1024,768]{0,1:T(8,128)S(1)}) fusion(f32[768]{0:T(1024)S(1)} %copy-done.58, bf16[1024,3072]{1,0:T(8,128)(2,1)} %get-tuple-element.347, bf16[3072,768]{1,0:T(8,128)(2,1)} %all-gather.12.cloned.1.call-done, f32[768]{0:T(1024)S(1)} %copy-done.56, f32[768]{0:T(1024)S(1)} %copy-done.44, f32[1024]{0:T(1024)S(1)} %fusion.44, ...), kind=kOutput, calls=%fused_computation.147 | convolution fusion | flops 4837342208 | bytes 17323008 | tf_op jit(solution)/shard_map/dot_general | solution.py:184
  289.3 3.3 convert_reduce_fusion.2
  292.6 18.0 %convert_reduce_fusion = (f32[3072]{0:T(1024)}, bf16[1024,3072]{1,0:T(8,128)(2,1)}) fusion(f32[1024,3072]{1,0:T(8,128)} %get-tuple-element.348, bf16[1024,768]{0,1:T(8,128)(2,1)S(1)} %get-tuple-element.338, bf16[3072,768]{1,0:T(8,128)(2,1)} %all-gather.12.cloned.1.call-done, f32[1024,3072]{1,0:T(8,128)} %get-tuple-element.358, f32[3072]{0:T(1024)S(1)} %copy-done.54), kind=kOutput, calls=%fused_computation.39 | convolution fusion | flops 4885312512 | bytes 37773312 | tf_op jit(solution)/shard_map/dot_general | solution.py:47
  310.6 11.4 %multiply_reduce_fusion.1 = (f32[768]{0:T(1024)}, f32[1024]{0:T(1024)S(1)}, f32[768]{0:T(1024)}, f32[1024,768]{0,1:T(8,128)S(1)}) fusion(f32[1024,768]{0,1:T(8,128)} %copy-done.10, f32[1024]{0:T(1024)S(1)} %fusion.44, f32[1024]{0:T(1024)S(1)} %broadcast_multiply_fusion.1, f32[768]{0:T(1024)S(1)} %copy-done.44, bf16[1024,3072]{1,0:T(8,128)(2,1)} %get-tuple-element.363, ...), kind=kOutput, calls=%fused_computation.65 | convolution fusion | flops 4845204480 | bytes 22061056 | tf_op jit(solution)/shard_map/dot_general | solution.py:47
  325.4 2.9 fusion.60
  328.4 3.9 convolution_convert_fusion
  333.7 175.4 %while.28 = (s32[]{:T(128)}, f32[1024,12,64]{0,2,1:T(8,128)}, f32[1024,12,64]{0,2,1:T(8,128)}, bf16[2,512,12,64]{1,3,2,0:T(8,128)(2,1)}, s32[2]{0:T(128)S(1)}, /...) while((s32[]{:T(128)}, f32[1024,12,64]{0,2,1:T(8,128)}, ...), condition=%wide.region_16.17_spmd.clone, body=%wide.region_14.16_spmd.clone.sunk | while | flops 4125747200 | bytes 225634640 | solution.py:114
  337.7 11.7 %fusion.124 = f32[12,512,1024]{2,1,0:T(8,128)} fusion(bf16[1024,12,64]{0,2,1:T(8,128)(2,1)S(1)} %get-tuple-element.581, bf16[1024,12,64]{0,2,1:T(8,128)(2,1)} %get-tuple-element.578, s32[]{:T(128)S(6)} %select_n.60), kind=kOutput, calls=%fused_computation.28.clone.1 | convolution fusion | flops 805306368 | bytes 27525124 | tf_op jit(solution)/shard_map/while/body/eval_jaxpr/qhd,khd->hqk/dot_general | solution.py:53
  349.4 13.6 %bitcast_add_fusion.5 = f32[1024,12,64]{0,2,1:T(8,128)} fusion(f32[1024,12,64]{0,2,1:T(8,128)} %get-tuple-element.558, f32[12,512,1024]{2,1,0:T(8,128)} %fusion.124, f32[12,512]{1,0:T(8,128)S(1)} %dynamic-slice_bitcast_fusion.2, pred[512,1024]{1,0:T(8,128)(4,1)S(1)} %broadcast_compare_fusion.5, pred[]{:T(512)S(6)} %compare.3, ...), kind=kOutput, calls=%fused_computation.20.clone.1 | convolution fusion | flops 832045056 | bytes 32800772 | tf_op jit(solution)/shard_map/while/body/eval_jaxpr/hqk,qhd->khd/dot_general | solution.py:105
  363.1 18.2 %multiply_reduce_fusion.11 = (f32[12,512]{1,0:T(8,128)S(1)}, f32[12,512,1024]{2,1,0:T(8,128)}) fusion(f32[12,512,1024]{2,1,0:T(8,128)} %fusion.124, f32[12,512]{1,0:T(8,128)S(1)} %dynamic-slice_bitcast_fusion.2, pred[512,1024]{1,0:T(8,128)(4,1)S(1)} %broadcast_compare_fusion.5, bf16[1024,12,64]{0,2,1:T(8,128)(2,1)} %get-tuple-element.584, ...), kind=kOutput, calls=%fused_computation.15.clone.1 | convolution fusion | flops 836757504 | bytes 53264388 | tf_op jit(solution)/shard_map/while/body/eval_jaxpr/qhd,khd->hqk/dot_general | solution.py:92
  381.3 21.9 %multiply_convert_fusion.3 = bf16[12,512,1024]{2,1,0:T(8,128)(2,1)} fusion(f32[12,512,1024]{2,1,0:T(8,128)} %get-tuple-element.498, f32[12,512,1024]{2,1,0:T(8,128)} %fusion.124, f32[12,512]{1,0:T(8,128)S(1)} %get-tuple-element.499, f32[12,512]{1,0:T(8,128)S(1)} %dynamic-slice_bitcast_fusion.2, pred[512,1024]{1,0:T(8,128)(4,1)S(1)} %broadcast_compare_fusion.5), kind=kLoop, calls=%fused_computation.14.clone.1 | loop fusion | flops 37748736 | bytes 63488000 | tf_op jit(solution)/shard_map/while/body/eval_jaxpr/convert_element_type | solution.py:98
  403.2 9.6 bitcast_dynamic-update-slice_fusion.8
  412.8 8.6 bitcast_add_fusion.4
  425.0 11.4 %fusion.124 = f32[12,512,1024]{2,1,0:T(8,128)} fusion(bf16[1024,12,64]{0,2,1:T(8,128)(2,1)S(1)} %get-tuple-element.581, bf16[1024,12,64]{0,2,1:T(8,128)(2,1)} %get-tuple-element.578, s32[]{:T(128)S(6)} %select_n.60), kind=kOutput, calls=%fused_computation.28.clone.1 | convolution fusion | flops 805306368 | bytes 27525124 | tf_op jit(solution)/shard_map/while/body/eval_jaxpr/qhd,khd->hqk/dot_general | solution.py:53
  436.4 14.2 %bitcast_add_fusion.5 = f32[1024,12,64]{0,2,1:T(8,128)} fusion(f32[1024,12,64]{0,2,1:T(8,128)} %get-tuple-element.558, f32[12,512,1024]{2,1,0:T(8,128)} %fusion.124, f32[12,512]{1,0:T(8,128)S(1)} %dynamic-slice_bitcast_fusion.2, pred[512,1024]{1,0:T(8,128)(4,1)S(1)} %broadcast_compare_fusion.5, pred[]{:T(512)S(6)} %compare.3, ...), kind=kOutput, calls=%fused_computation.20.clone.1 | convolution fusion | flops 832045056 | bytes 32800772 | tf_op jit(solution)/shard_map/while/body/eval_jaxpr/hqk,qhd->khd/dot_general | solution.py:105
  450.6 18.1 %multiply_reduce_fusion.11 = (f32[12,512]{1,0:T(8,128)S(1)}, f32[12,512,1024]{2,1,0:T(8,128)}) fusion(f32[12,512,1024]{2,1,0:T(8,128)} %fusion.124, f32[12,512]{1,0:T(8,128)S(1)} %dynamic-slice_bitcast_fusion.2, pred[512,1024]{1,0:T(8,128)(4,1)S(1)} %broadcast_compare_fusion.5, bf16[1024,12,64]{0,2,1:T(8,128)(2,1)} %get-tuple-element.584, ...), kind=kOutput, calls=%fused_computation.15.clone.1 | convolution fusion | flops 836757504 | bytes 53264388 | tf_op jit(solution)/shard_map/while/body/eval_jaxpr/qhd,khd->hqk/dot_general | solution.py:92
  468.7 21.2 %multiply_convert_fusion.3 = bf16[12,512,1024]{2,1,0:T(8,128)(2,1)} fusion(f32[12,512,1024]{2,1,0:T(8,128)} %get-tuple-element.498, f32[12,512,1024]{2,1,0:T(8,128)} %fusion.124, f32[12,512]{1,0:T(8,128)S(1)} %get-tuple-element.499, f32[12,512]{1,0:T(8,128)S(1)} %dynamic-slice_bitcast_fusion.2, pred[512,1024]{1,0:T(8,128)(4,1)S(1)} %broadcast_compare_fusion.5), kind=kLoop, calls=%fused_computation.14.clone.1 | loop fusion | flops 37748736 | bytes 63488000 | tf_op jit(solution)/shard_map/while/body/eval_jaxpr/convert_element_type | solution.py:98
  490.0 9.5 bitcast_dynamic-update-slice_fusion.8
  499.5 9.5 bitcast_add_fusion.4
  513.5 2.7 convert_reduce_fusion.4
  520.6 3.3 pad_maximum_fusion
  523.9 11.0 %copy.117 = f32[3,768,768]{2,0,1:T(4,128)} copy(f32[3,768,768]{1,2,0:T(8,128)} %pad_maximum_fusion) | data formatting | bytes 14155776 | tf_op jit(solution)/shard_map/stack | solution.py:218
  535.7 10.6 fusion.46
  546.3 10.3 fusion.61
  560.5 41.2 %all-reduce.1 = f32[12,768]{1,0:T(8,128)S(1)} all-reduce(f32[12,768]{1,0:T(8,128)S(1)} %concatenate.3), channel_id=6, replica_groups=mesh['dp'=4,'fsdp'=8] {'dp','fsdp'}, use_global_device_ids=true, to_apply=%region_34.35.clone | all-reduce | flops 9216 | bytes 73728
  602.4 3.3 fusion.37
  611.0 115.4 %all-reduce.4.cloned.1.call-done = f32[3,768,768]{2,0,1:T(4,128)} async-done(((f32[3,768,768]{2,0,1:T(4,128)}), f32[3,768,768]{2,0,1:T(4,128)}) %all-reduce.4.cloned.1.call-update) | async-done | bytes 7077904
  729.4 138.6 %reduce-scatter.7.cloned.1.call-done = f32[24,3072]{1,0:T(8,128)} async-done(((f32[768,3072]{1,0:T(8,128)}), f32[24,3072]{1,0:T(8,128)}) %reduce-scatter.7.cloned.1.call-update) | async-done | bytes 294928 | tf_op jit(solution)/shard_map/reduce_scatter | solution.py:247
  870.3 139.0 %reduce-scatter.9.cloned.1.call-done = f32[96,768]{1,0:T(8,128)} async-done(((f32[3072,768]{1,0:T(8,128)}), f32[96,768]{1,0:T(8,128)}) %reduce-scatter.9.cloned.1.call-update) | async-done | bytes 294928 | tf_op jit(solution)/shard_map/reduce_scatter | solution.py:248
  1013.9 40.0 %psum.7 = f32[]{:T(128)} all-reduce(f32[]{:T(128)S(6)} %add.281), channel_id=1, replica_groups=mesh['dp'=4,'fsdp'=8] {'dp','fsdp'}, use_global_device_ids=true, to_apply=%region_36.37 | all-reduce | flops 1 | bytes 8 | tf_op jit(solution)/shard_map/psum | solution.py:258
  (231 shorter events, 65.1 us)
Async XLA Ops:
  7.2 54.2 %copy-start.13 = (bf16[1024,768]{1,0:T(8,128)(2,1)S(1)}, bf16[1024,768]{1,0:T(8,128)(2,1)}, u32[]{:S(2)}) copy-start(bf16[1024,768]{1,0:T(8,128)(2,1)} %param.23) | copy-start | bytes 4718596
  7.2 55.8 %copy-start.14 = (bf16[1024,768]{1,0:T(8,128)(2,1)S(1)}, bf16[1024,768]{1,0:T(8,128)(2,1)}, u32[]{:S(2)}) copy-start(bf16[1024,768]{1,0:T(8,128)(2,1)} %param.22) | copy-start | bytes 4718596
  7.2 67.7 %all-gather.6.cloned.1.call-start = ((), (), s32[]{:S(2)}) async-start(), calls=%async_computation.3 | async-start | bytes 3649536 | tf_op jit(solution)/shard_map/all_gather | solution.py:152
  9.0 153.0 %all-gather.8.cloned.1.call-start = ((), (), s32[]{:S(2)}) async-start(), calls=%async_computation.4 | async-start | bytes 1216512 | tf_op jit(solution)/shard_map/all_gather | solution.py:153
  10.6 187.2 %all-gather.10.cloned.1.call-start = ((), (), s32[]{:S(2)}) async-start(), calls=%async_computation.5 | async-start | bytes 4866048 | tf_op jit(solution)/shard_map/all_gather | solution.py:154
  12.3 251.4 %all-gather.12.cloned.1.call-start = ((), (), s32[]{:S(2)}) async-start(), calls=%async_computation.6 | async-start | bytes 4866048 | tf_op jit(solution)/shard_map/all_gather | solution.py:155
  14.0 595.3 %reduce-scatter.5.cloned.1.call-start = ((), (), s32[]{:S(2)}) async-start(), calls=%async_computation.7 | async-start | bytes 2433024 | tf_op jit(solution)/shard_map/reduce_scatter | solution.py:246
  85.0 22.9 %copy-start.5 = (bf16[1024,12,64]{0,2,1:T(8,128)(2,1)S(1)}, bf16[1024,12,64]{0,2,1:T(8,128)(2,1)}, u32[]{:S(2)}) copy-start(bf16[1024,12,64]{0,2,1:T(8,128)(2,1)} %get-tuple-element.534) | copy-start | bytes 4718596 | tf_op jit(solution)/shard_map/while
  95.5 15.4 %copy-start = (f32[12,512,1024]{2,1,0:T(8,128)S(1)}, f32[12,512,1024]{2,1,0:T(8,128)}, u32[]{:S(2)}) copy-start(f32[12,512,1024]{2,1,0:T(8,128)} %get-tuple-element.484) | copy-start | bytes 75497472 | tf_op jit(solution)/shard_map/while
  121.2 23.0 %copy-start.5 = (bf16[1024,12,64]{0,2,1:T(8,128)(2,1)S(1)}, bf16[1024,12,64]{0,2,1:T(8,128)(2,1)}, u32[]{:S(2)}) copy-start(bf16[1024,12,64]{0,2,1:T(8,128)(2,1)} %get-tuple-element.534) | copy-start | bytes 4718596 | tf_op jit(solution)/shard_map/while
  131.9 15.5 %copy-start = (f32[12,512,1024]{2,1,0:T(8,128)S(1)}, f32[12,512,1024]{2,1,0:T(8,128)}, u32[]{:S(2)}) copy-start(f32[12,512,1024]{2,1,0:T(8,128)} %get-tuple-element.484) | copy-start | bytes 75497472 | tf_op jit(solution)/shard_map/while
  156.2 5.8 copy-start.1
  156.2 5.8 copy-start.3
  156.2 5.8 copy-start.26
  156.2 5.8 copy-start.29
  156.2 5.8 copy-start.59
  165.9 69.5 %copy-start.10 = (f32[1024,768]{0,1:T(8,128)}, f32[1024,768]{0,1:T(8,128)S(1)}, u32[]{:S(2)}) copy-start(f32[1024,768]{0,1:T(8,128)S(1)} %get-tuple-element.357) | copy-start | bytes 9437188
  165.9 31.9 %copy-start.44 = (f32[768]{0:T(1024)S(1)}, f32[768]{0:T(1024)}, u32[]{:S(2)}) copy-start(f32[768]{0:T(1024)} %get-tuple-element.276) | copy-start | bytes 9220
  165.9 31.9 %copy-start.54 = (f32[3072]{0:T(1024)S(1)}, f32[3072]{0:T(1024)}, u32[]{:S(2)}) copy-start(f32[3072]{0:T(1024)} %add.263) | copy-start | bytes 36868
  165.9 31.9 %copy-start.56 = (f32[768]{0:T(1024)S(1)}, f32[768]{0:T(1024)}, u32[]{:S(2)}) copy-start(f32[768]{0:T(1024)} %get-tuple-element.275) | copy-start | bytes 9220
  165.9 156.1 %copy-start.41 = (f32[1024]{0:T(1024)}, f32[1024]{0:T(1024)S(1)}, u32[]{:S(2)}) copy-start(f32[1024]{0:T(1024)S(1)} %broadcast_multiply_fusion.1) | copy-start | bytes 12292
  166.3 155.7 %copy-start.50 = (f32[1024]{0:T(1024)}, f32[1024]{0:T(1024)S(1)}, u32[]{:S(2)}) copy-start(f32[1024]{0:T(1024)S(1)} %fusion.44) | copy-start | bytes 12292
  197.8 65.9 %copy-start.58 = (f32[768]{0:T(1024)S(1)}, f32[768]{0:T(1024)}, u32[]{:S(2)}) copy-start(f32[768]{0:T(1024)} %get-tuple-element.274) | copy-start | bytes 9220
  263.7 21.7 %copy-start.8 = (bf16[1024,768]{0,1:T(8,128)(2,1)S(1)}, bf16[1024,768]{0,1:T(8,128)(2,1)}, u32[]{:S(2)}) copy-start(bf16[1024,768]{0,1:T(8,128)(2,1)} %copy.111) | copy-start | bytes 4718596
  263.7 21.7 %copy-start.38 = (f32[768]{0:T(1024)S(1)}, f32[768]{0:T(1024)}, u32[]{:S(2)}) copy-start(f32[768]{0:T(1024)} %get-tuple-element.272) | copy-start | bytes 9220
  292.6 18.0 %copy-start.19 = (bf16[1024,768]{0,1:T(8,128)(2,1)}, bf16[1024,768]{0,1:T(8,128)(2,1)S(1)}, u32[]{:S(2)}) copy-start(bf16[1024,768]{0,1:T(8,128)(2,1)S(1)} %get-tuple-element.338) | copy-start | bytes 4718596
  310.6 11.4 %copy-start.11 = (f32[1024,768]{0,1:T(8,128)S(1)}, f32[1024,768]{0,1:T(8,128)}, u32[]{:S(2)}) copy-start(f32[1024,768]{0,1:T(8,128)} %copy-done.10) | copy-start | bytes 9437188
  328.4 5.3 copy-start.2
  328.4 398.0 %all-reduce.4.cloned.1.call-start = ((), (), s32[]{:S(2)}) async-start(), calls=%async_computation.10 | async-start | bytes 18874368
  337.7 11.7 %copy-start.12 = (bf16[1024,12,64]{0,2,1:T(8,128)(2,1)S(1)}, bf16[1024,12,64]{0,2,1:T(8,128)(2,1)}, u32[]{:S(2)}) copy-start(bf16[1024,12,64]{0,2,1:T(8,128)(2,1)} %get-tuple-element.583) | copy-start | bytes 4718596 | tf_op jit(solution)/shard_map/while
  403.2 9.6 copy-start.4
  425.0 11.4 %copy-start.12 = (bf16[1024,12,64]{0,2,1:T(8,128)(2,1)S(1)}, bf16[1024,12,64]{0,2,1:T(8,128)(2,1)}, u32[]{:S(2)}) copy-start(bf16[1024,12,64]{0,2,1:T(8,128)(2,1)} %get-tuple-element.583) | copy-start | bytes 4718596 | tf_op jit(solution)/shard_map/while
  490.0 9.5 copy-start.4
  511.4 7.9 copy-start.20
  535.0 333.0 %reduce-scatter.7.cloned.1.call-start = ((), (), s32[]{:S(2)}) async-start(), calls=%async_computation.8 | async-start | bytes 9732096 | tf_op jit(solution)/shard_map/reduce_scatter | solution.py:247
  546.3 463.1 %reduce-scatter.9.cloned.1.call-start = ((), (), s32[]{:S(2)}) async-start(), calls=%async_computation.9 | async-start | bytes 9732096 | tf_op jit(solution)/shard_map/reduce_scatter | solution.py:248
  609.3 445.4 %copy-start.43 = (f32[12,24]{1,0:T(8,128)S(1)}, f32[12,24]{1,0:T(8,128)}, u32[]{:S(2)}) copy-start(f32[12,24]{1,0:T(8,128)} %param.29) | copy-start | bytes 3460
  609.3 445.4 %copy-start.55 = (f32[12,24]{1,0:T(8,128)S(1)}, f32[12,24]{1,0:T(8,128)}, u32[]{:S(2)}) copy-start(f32[12,24]{1,0:T(8,128)} %param.34) | copy-start | bytes 3460
  609.3 446.8 %copy-start.28 = (f32[3,24,768]{2,1,0:T(8,128)S(1)}, f32[3,24,768]{2,1,0:T(8,128)}, u32[]{:S(2)}) copy-start(f32[3,24,768]{2,1,0:T(8,128)} %param.25) | copy-start | bytes 663556
  609.3 448.8 %copy-start.35 = (f32[24,768]{1,0:T(8,128)S(1)}, f32[24,768]{1,0:T(8,128)}, u32[]{:S(2)}) copy-start(f32[24,768]{1,0:T(8,128)} %param.26) | copy-start | bytes 221188
  609.3 448.8 %copy-start.37 = (f32[24,768]{1,0:T(8,128)S(1)}, f32[24,768]{1,0:T(8,128)}, u32[]{:S(2)}) copy-start(f32[24,768]{1,0:T(8,128)} %param.31) | copy-start | bytes 221188
  609.4 448.7 %copy-start.36 = (f32[24,768]{1,0:T(8,128)S(1)}, f32[24,768]{1,0:T(8,128)}, u32[]{:S(2)}) copy-start(f32[24,768]{1,0:T(8,128)} %reduce-scatter.5.cloned.1.call-done) | copy-start | bytes 221188
  611.0 448.7 %copy-start.22 = (f32[96,768]{1,0:T(8,128)S(1)}, f32[96,768]{1,0:T(8,128)}, u32[]{:S(2)}) copy-start(f32[96,768]{1,0:T(8,128)} %param.28) | copy-start | bytes 884740
  1009.3 50.4 %copy-start.25 = (f32[96,768]{1,0:T(8,128)S(1)}, f32[96,768]{1,0:T(8,128)}, u32[]{:S(2)}) copy-start(f32[96,768]{1,0:T(8,128)} %reduce-scatter.9.cloned.1.call-done) | copy-start | bytes 884740
  1012.3 49.5 %copy-start.23 = (f32[24,3072]{1,0:T(8,128)S(1)}, f32[24,3072]{1,0:T(8,128)}, u32[]{:S(2)}) copy-start(f32[24,3072]{1,0:T(8,128)} %param.27) | copy-start | bytes 884740
  1012.4 49.5 %copy-start.24 = (f32[24,3072]{1,0:T(8,128)S(1)}, f32[24,3072]{1,0:T(8,128)}, u32[]{:S(2)}) copy-start(f32[24,3072]{1,0:T(8,128)} %reduce-scatter.7.cloned.1.call-done) | copy-start | bytes 884740
  1013.9 47.9 %copy-start.33 = (f32[24,3072]{1,0:T(8,128)S(1)}, f32[24,3072]{1,0:T(8,128)}, u32[]{:S(2)}) copy-start(f32[24,3072]{1,0:T(8,128)} %param.32) | copy-start | bytes 884740
  1013.9 47.9 %copy-start.34 = (f32[24,3072]{1,0:T(8,128)S(1)}, f32[24,3072]{1,0:T(8,128)}, u32[]{:S(2)}) copy-start(f32[24,3072]{1,0:T(8,128)} %param.37) | copy-start | bytes 884740
  (26 other events, 56.0 us)
Sparse Core Ops, SparseCore 0:
  11.8 63.0 all-gather.5
  78.5 53.0 all-gather.7
  135.2 62.5 all-gather.9
  201.2 62.4 all-gather.11
  328.5 97.8 reduce-scatter.4
  535.1 191.2 all-reduce.3
  732.3 135.6 reduce-scatter.6
  874.9 134.3 reduce-scatter.8
where the time goes:
time: 1080 us; the launch traced here: 1070 us
  waiting for transfers between devices  463 us (43%)
  matrix products  300 us (28%)
  blocking collectives  125 us (12%)
  other arithmetic  111 us (10%)
  local copies, waits for them, and re-layouts  43.8 us (4%)
  between operations  20.2 us (2%)
    reduce_scatter x1, waiting for transfers between devices, per_device(): lax.psum_scatter(grad_down, ('dp', 'fsdp'), scatter_dimension=0, tiled=True)  139 us
    reduce_scatter x1, waiting for transfers between devices, per_device(): lax.psum_scatter(grad_in, ('dp', 'fsdp'), scatter_dimension=0, tiled=True)  139 us
    unnamed x9, waiting for transfers between devices  116 us
    dot_general x4, matrix products, masked_scores(): jnp.einsum('qhd,khd->hqk', query_block, key_heads, preferred_element_type...  44.3 us
    all_gather x1, blocking collectives, per_device(): lax.all_gather(vectors.astype(jnp.bfloat16), ('dp', 'fsdp'), axis=1, tile...  44 us
    convert_element_type x2, other arithmetic, one_block(): score_low = grad_scores.astype(jnp.bfloat16)  43.1 us
    unnamed x1, blocking collectives  41.2 us
    psum x1, blocking collectives, per_device(): total_sum = lax.psum(local_squares, ('dp', 'fsdp'))  40 us
  transfers between devices with their start and end apart: 8, of which 6 were waited for; matrix products, arithmetic and copies ran while one was open for 34% of the time, Pallas kernels for 0%

commit v1 on v0

v1 whole, which is shorter than its diff:
```python
import functools

import jax
import jax.numpy as jnp
from jax import lax
from jax.experimental import pallas as pl
from jax.experimental.pallas import tpu as pltpu
from jax.sharding import PartitionSpec as P

D = 768
H = 12
HD = 64
FF = 3072
T = 1024
STEP = 10
PAIRS = H // 2
W3 = 384

moment_decay = 0.9
square_decay = 0.999
learn_rate = 0.02
vector_rate = 0.15
weight_decay = 0.01
adam_epsilon = 1e-08
clip_limit = 1.0
norm_epsilon = 1e-05

bf = jnp.bfloat16
f32 = jnp.float32
MESH = pl.DeviceIdType.MESH
VM = pl.BlockSpec(memory_space=pltpu.VMEM)
ANY = pl.BlockSpec(memory_space=pl.ANY)
MIB = 2**20


def S(shape, dtype):
    return jax.ShapeDtypeStruct(shape, dtype)


def nn(a, b):
    return lax.dot_general(a, b, (((1,), (0,)), ((), ())), preferred_element_type=f32)


def nt(a, b):
    return lax.dot_general(a, b, (((1,), (1,)), ((), ())), preferred_element_type=f32)


def tn(a, b):
    return lax.dot_general(a, b, (((0,), (0,)), ((), ())), preferred_element_type=f32)


def colsum(x):
    return jnp.sum(x, axis=0, keepdims=True)


class Place:
    def __init__(self):
        self.dp = lax.axis_index("dp")
        self.fs = lax.axis_index("fsdp")
        self.z = self.fs // 2
        self.k = self.fs % 2
        dp, k = self.dp, self.k
        xn = dp + 1 - 2 * (dp % 2)
        yn = (dp + 2) % 4
        self.dp1 = xn * (1 - k) + yn * k
        self.dp2 = yn * (1 - k) + xn * k
        self.dp3 = 3 - dp
        self.n1 = (self.dp1, self.fs)
        self.n2 = (self.dp2, self.fs)
        self.sib = (dp, self.z * 2 + 1 - k)
        self.zp = [(dp, ((self.z + i) % 4) * 2 + k) for i in (1, 2, 3)]
        self.m = dp * 2 + k
        self.others = []
        for j in range(1, 8):
            other = (self.m + j) % 8
            self.others.append((other // 2, self.z * 2 + other % 2))


def enter(peers):
    barrier = pltpu.get_barrier_semaphore()
    for peer in peers:
        pl.semaphore_signal(barrier, inc=1, device_id=peer, device_id_type=MESH)
    pl.semaphore_wait(barrier, len(peers))


def rcopy(src, dst, ssem, rsem, peer):
    return pltpu.make_async_remote_copy(src, dst, ssem, rsem, device_id=peer, device_id_type=MESH)


def gather_kernel(
    qkv, out, inw, down, vec, wqkv, wo, wi, w2, vt,
    sx_qkv, sx_out, sx_in, sx_down, sx_vec, myvec, own_qkv, own_out, own_in, own_down, own_vec,
    xs, xr, gs, gr, ls,
):
    p = Place()
    k = p.k
    enter([p.sib, p.n1, p.n2] + p.zp)
    pad = jnp.concatenate([vec[...], jnp.zeros((128 - 12, 24), f32)], axis=0)
    myvec[...] = jnp.concatenate([pad, jnp.zeros((128, 104), f32)], axis=1).T[:24, :]
    half = lambda w, c: pl.ds(pl.multiple_of(c * w, 128), w)
    far = 1 - k
    swaps = [
        rcopy(qkv.at[:, :, half(W3, far)], sx_qkv, xs.at[0], xr.at[0], p.sib),
        rcopy(myvec, sx_vec, xs.at[4], xr.at[4], p.sib),
        rcopy(out.at[:, half(W3, far)], sx_out, xs.at[1], xr.at[1], p.sib),
        rcopy(inw.at[:, half(4 * W3, far)], sx_in, xs.at[2], xr.at[2], p.sib),
        rcopy(down.at[:, half(W3, far)], sx_down, xs.at[3], xr.at[3], p.sib),
    ]
    for c in swaps:
        c.start()
    for c in swaps:
        c.wait()

    def both(mine, other):
        lo = jnp.where(k == 0, mine, other)
        hi = jnp.where(k == 0, other, mine)
        return jnp.concatenate([lo, hi], axis=0).astype(bf)

    for j in range(3):
        mat = both(qkv[j, :, half(W3, k)], sx_qkv[j])
        for t in range(3):
            own_qkv[:, t * W3 + j * 128 : t * W3 + (j + 1) * 128] = mat[:, t * 128 : (t + 1) * 128]
    own_vec[...] = both(myvec[...], sx_vec[...])
    own_out[...] = both(out[:, half(W3, k)], sx_out[...])
    own_in[...] = both(inw[:, half(4 * W3, k)], sx_in[...])
    own_down[...] = both(down[:, half(W3, k)], sx_down[...])
    chip = p.dp * 4 + p.z
    rows48 = pl.ds(pl.multiple_of(chip * 48, 16), 48)
    rows192 = pl.ds(pl.multiple_of(chip * 192, 16), 192)
    local = [
        pltpu.make_async_copy(own_qkv, wqkv.at[rows48, half(3 * W3, k)], ls.at[0]),
        pltpu.make_async_copy(own_out, wo.at[rows48, half(W3, k)], ls.at[1]),
        pltpu.make_async_copy(own_in, wi.at[rows48, half(4 * W3, k)], ls.at[2]),
        pltpu.make_async_copy(own_down, w2.at[rows192, half(W3, k)], ls.at[3]),
        pltpu.make_async_copy(own_vec, vt.at[rows48, :], ls.at[4]),
    ]
    for c in local:
        c.start()
    for c in local:
        c.wait()

    chunks = [(vt, 48, pl.ds(0, 128))]
    for t in range(3):
        chunks.append((wqkv, 48, pl.ds(pl.multiple_of((t + 3 * k) * W3, 128), W3)))
    chunks.append((wo, 48, pl.ds(pl.multiple_of(k * W3, 128), W3)))
    for t in range(4):
        chunks.append((wi, 48, pl.ds(pl.multiple_of((t + 4 * k) * W3, 128), W3)))
    for t in range(3):
        chunks.append((w2, 192, pl.ds(pl.multiple_of(k * W3 + t * 128, 128), 128)))

    def rowsof(rc, dp, z=None):
        if z is None:
            return pl.ds(pl.multiple_of(dp * 4 * rc, 16), 4 * rc)
        return pl.ds(pl.multiple_of((dp * 4 + z) * rc, 16), rc)

    def same(i, j, rows, peer):
        ref, rc, cols = chunks[i]
        view = ref.at[rows, cols]
        return rcopy(view, view, gs.at[i, j], gr.at[i, j], peer)

    sent = []

    def go(c):
        c.start()
        sent.append(c)
        return c

    n = len(chunks)
    zc, c1, c2, c3, c4 = {}, {}, {}, {}, {}
    for s in range(n + 4):
        if s < n:
            rc = chunks[s][1]
            zc[s] = [go(same(s, i, rowsof(rc, p.dp, p.z), p.zp[i])) for i in range(3)]
        i = s - 1
        if 0 <= i < n:
            rc = chunks[i][1]
            for c in zc[i]:
                c.wait_recv()
            c1[i] = go(same(i, 3, rowsof(rc, p.dp), p.n1))
            c2[i] = go(same(i, 4, rowsof(rc, p.dp), p.n2))
        i = s - 2
        if 0 <= i < n:
            rc = chunks[i][1]
            c1[i].wait_recv()
            c3[i] = go(same(i, 5, rowsof(rc, p.dp1), p.n2))
        i = s - 3
        if 0 <= i < n:
            rc = chunks[i][1]
            c2[i].wait_recv()
            c3[i].wait_recv()
            if i > 0:
                c4[i] = go(same(i, 6, pl.ds(0, 16 * rc), p.sib))
        i = s - 4
        if 0 < i < n:
            c4[i].wait_recv()
    for c in sent:
        c.wait_send()


def gather_weights(qkv, out, inw, down, vec):
    return pl.pallas_call(
        gather_kernel,
        in_specs=[VM] * 5,
        out_specs=[ANY] * 5,
        out_shape=[S((D, 3 * D), bf), S((D, D), bf), S((D, FF), bf), S((FF, D), bf), S((D, 128), bf)],
        scratch_shapes=[
            pltpu.VMEM((3, 24, W3), f32), pltpu.VMEM((24, W3), f32), pltpu.VMEM((24, 4 * W3), f32),
            pltpu.VMEM((96, W3), f32), pltpu.VMEM((24, 128), f32), pltpu.VMEM((24, 128), f32),
            pltpu.VMEM((48, 3 * W3), bf), pltpu.VMEM((48, W3), bf), pltpu.VMEM((48, 4 * W3), bf),
            pltpu.VMEM((192, W3), bf), pltpu.VMEM((48, 128), bf),
            pltpu.SemaphoreType.DMA((5,)), pltpu.SemaphoreType.DMA((5,)),
            pltpu.SemaphoreType.DMA((12, 7)), pltpu.SemaphoreType.DMA((12, 7)), pltpu.SemaphoreType.DMA((5,)),
        ],
        compiler_params=pltpu.CompilerParams(collective_id=0, has_side_effects=True, vmem_limit_bytes=40 * MIB),
        name="gather_weights",
    )(qkv, out, inw, down, vec)


def forward_kernel(block, tok, w, bias, onehot, neg, q_o, k_o, v_o, ctx_o, lse_o, qa, ka, va):
    lane = lax.broadcasted_iota(jnp.int32, (1, 128), 1)
    y = nn(tok[...], w[...]) + bias[...]
    q = y[:, :128].astype(bf)
    key = y[:, 128:256].astype(bf)
    val = y[:, 256:].astype(bf)
    q_o[...] = q
    k_o[...] = key
    v_o[...] = val
    qs = (q.astype(f32) * HD ** (-0.5)).astype(bf)
    ka[:, :128] = key
    ka[:, 128:] = neg[...]
    va[:, :128] = val
    va[:, 128:] = jnp.ones((T, 128), bf)
    qa[:, 128:] = onehot[...]
    for h in range(2):
        sel = (lane // 64) == h
        qa[:, :128] = jnp.where(sel, qs, jnp.zeros_like(qs))
        for b in range(T // block):
            r = slice(b * block, (b + 1) * block)
            s = nt(qa[r, :], ka[...])
            m = jnp.max(s, axis=1, keepdims=True)
            e = jnp.exp(s - m).astype(bf)
            o = nn(e, va[...])
            tot = o[:, 128:]
            c = o[:, :128] / tot
            l = m + jnp.log(tot)
            if h == 0:
                ctx_o[r, :] = c
                lse_o[0, r, :] = l
            else:
                ctx_o[r, :] = jnp.where(sel, c, ctx_o[r, :])
                lse_o[0, r, :] = jnp.where(lane == 1, l, lse_o[0, r, :])


def attend(tok, w, bias, onehot, neg, block=256):
    full = lambda s: pl.BlockSpec(s, lambda i: (0,) * len(s))
    col = pl.BlockSpec((T, 128), lambda i: (0, i))
    return pl.pallas_call(
        functools.partial(forward_kernel, block),
        grid=(PAIRS,),
        in_specs=[
            full((T, D)), pl.BlockSpec((D, W3), lambda i: (0, i)), pl.BlockSpec((1, W3), lambda i: (0, i)),
            full((T, 128)), full((T, 128)),
        ],
        out_specs=[col, col, col, col, pl.BlockSpec((1, T, 128), lambda i: (i, 0, 0))],
        out_shape=[S((T, D), bf)] * 3 + [S((T, D), f32), S((PAIRS, T, 128), f32)],
        scratch_shapes=[pltpu.VMEM((T, 256), bf)] * 3,
        compiler_params=pltpu.CompilerParams(vmem_limit_bytes=50 * MIB),
        name="attend",
    )(tok, w, bias, onehot, neg)


def split3(x):
    hi = x.astype(bf).astype(f32)
    mid = (x - hi).astype(bf).astype(f32)
    return hi, mid, x - hi - mid


def backward_kernel(
    block, tok, w, dh1, q_i, k_i, v_i, dctx_i, ctx_i, lse_i, onehot, neg,
    g_o, ig_o, vg_o, qa, ka, va, da, kT, dqT, dka, dva, tokT, ig,
):
    lane = lax.broadcasted_iota(jnp.int32, (1, 128), 1)
    step = pl.program_id(0)

    @pl.when(step == 0)
    def _():
        tokT[...] = tok[...].T
        ig[...] = dh1[...]

    key = k_i[...]
    val = v_i[...]
    qs = (q_i[...].astype(f32) * HD ** (-0.5)).astype(bf)
    minus = jnp.where((lane >= 16) & (lane < 19), -1.0, 0.0)
    ka[:, :128] = key
    ka[:, 128:] = (neg[...].astype(f32) + minus).astype(bf)
    va[:, :128] = val
    va[:, 128:] = jnp.broadcast_to(minus, (T, 128)).astype(bf)
    kT[...] = key.T
    d = dctx_i[...]
    prod = d.astype(f32) * ctx_i[...]
    for h in range(2):
        sel = (lane // 64) == h
        inner = jnp.sum(jnp.where(sel, prod, 0.0), axis=1, keepdims=True)
        lse = jnp.sum(jnp.where(lane == h, lse_i[0], 0.0), axis=1, keepdims=True)

        def extra(base, parts):
            for j, part in enumerate(parts):
                base = jnp.where(lane == 16 + j, part, base)
            return base.astype(bf)

        qa[:, :128] = jnp.where(sel, qs, jnp.zeros_like(qs))
        qa[:, 128:] = extra(onehot[...].astype(f32), split3(lse))
        da[:, :128] = jnp.where(sel, d, jnp.zeros_like(d))
        da[:, 128:] = extra(jnp.zeros((T, 128), f32), split3(inner))
        for b in range(T // block):
            r = slice(b * block, (b + 1) * block)
            pt = jnp.exp(nt(ka[...], qa[r, :]))
            dpt = nt(va[...], da[r, :])
            ds = (pt * dpt).astype(bf)
            x = nn(pt.astype(bf), da[r, :128])
            y = nn(ds, qa[r, :128])
            dqT[h * 64 : (h + 1) * 64, r] = nn(kT[h * 64 : (h + 1) * 64, :], ds)
            if h == 0 and b == 0:
                dva[...] = x
                dka[...] = y
            else:
                dva[...] += x
                dka[...] += y
    dv = dva[...].astype(bf)
    dk = dka[...].astype(bf)
    dq = (dqT[...].T * HD ** (-0.5)).astype(bf)
    vg_o[...] = jnp.zeros_like(vg_o)
    vg_o[0:1, :] = colsum(dq.astype(f32))
    vg_o[1:2, :] = colsum(dv.astype(f32))
    cat = jnp.concatenate([dq, dk, dv], axis=1)
    g_o[...] = nn(tokT[...], cat).astype(bf)
    ig[...] += nt(cat, w[...])

    @pl.when(step == PAIRS - 1)
    def _():
        ig_o[...] = ig[...].astype(bf)


def attend_back(tok, w, dh1, q, k, v, dctx, ctx, lse, onehot, neg, block=512):
    full = lambda s: pl.BlockSpec(s, lambda i: (0,) * len(s))
    col = pl.BlockSpec((T, 128), lambda i: (0, i))
    return pl.pallas_call(
        functools.partial(backward_kernel, block),
        grid=(PAIRS,),
        in_specs=[
            full((T, D)), pl.BlockSpec((D, W3), lambda i: (0, i)), full((T, D)),
            col, col, col, col, col, pl.BlockSpec((1, T, 128), lambda i: (i, 0, 0)), full((T, 128)), full((T, 128)),
        ],
        out_specs=[pl.BlockSpec((D, W3), lambda i: (0, i)), full((T, D)), pl.BlockSpec((16, 128), lambda i: (0, i))],
        out_shape=[S((D, 3 * D), bf), S((T, D), bf), S((16, D), f32)],
        scratch_shapes=[pltpu.VMEM((T, 256), bf)] * 4
        + [pltpu.VMEM((128, T), bf), pltpu.VMEM((128, T), f32)]
        + [pltpu.VMEM((T, 128), f32)] * 2
        + [pltpu.VMEM((D, T), bf), pltpu.VMEM((T, D), f32)],
        compiler_params=pltpu.CompilerParams(vmem_limit_bytes=56 * MIB),
        name="attend_back",
    )(tok, w, dh1, q, k, v, dctx, ctx, lse, onehot, neg)


def gelu_parts(x):
    e = jnp.exp(x * x * (-0.5))
    t = 1.0 / (1.0 + (0.3275911 * 0.7071067811865476) * jnp.abs(x))
    poly = 0.5 * 1.061405429
    for a in (-1.453152027, 1.421413741, -0.284496736, 0.254829592):
        poly = 0.5 * a + t * poly
    tail = t * poly * e
    return jnp.where(x >= 0, 1.0 - tail, tail), e * 0.3989422804014327


def norm_forward(h):
    c = h - jnp.mean(h, axis=1, keepdims=True)
    r = lax.rsqrt(jnp.mean(c * c, axis=1, keepdims=True) + norm_epsilon)
    return c * r, r


def norm_backward(dy, xh, r, g):
    dx = dy * g
    return r * (dx - jnp.mean(dx, axis=1, keepdims=True) - xh * jnp.mean(dx * xh, axis=1, keepdims=True))


def ffn_kernel(
    block, tok, ctx, cot, vec, wo_h, wi_h, w2_h, out_o, dh1_o, dctx_o, vg_o, gwo_h, gwi_h, gw2_h,
    wo, wi, w2, cb, x1b, hb, gp, dfb, dhp, dab, stage, tr, insem, outsem,
):
    loads = [
        pltpu.make_async_copy(wo_h, wo, insem.at[0]),
        pltpu.make_async_copy(wi_h, wi, insem.at[1]),
        pltpu.make_async_copy(w2_h, w2, insem.at[2]),
    ]
    for c in loads:
        c.start()
    vg_o[...] = jnp.zeros_like(vg_o)
    row = lambda i: vec[i : i + 1, :]
    for c in loads:
        c.wait()

    def one_block(b, carry):
        r = pl.ds(pl.multiple_of(b * block, block), block)
        c = ctx[r, :].astype(bf)
        cb[r, :] = c
        xh1, r1 = norm_forward(tok[r, :].astype(f32) + (nn(c, wo[...]) + row(2)))
        x1 = xh1 * row(4) + row(5)
        xb = x1.astype(bf)
        x1b[r, :] = xb
        acc = x1 + row(3)
        for j in range(4):
            cs = slice(j * D, (j + 1) * D)
            hp = nn(xb, wi[:, cs]) + row(8 + j)
            big, dense = gelu_parts(hp)
            h = (hp * big).astype(bf)
            hb[r, cs] = h
            gp[:, cs] = big + hp * dense
            acc = acc + nn(h, w2[cs, :])
        xh2, r2 = norm_forward(acc)
        out_o[r, :] = (xh2 * row(6) + row(7)).astype(bf)
        dy = cot[r, :].astype(f32)
        vg_o[6:7, :] += colsum(dy * xh2)
        vg_o[7:8, :] += colsum(dy)
        dh2 = norm_backward(dy, xh2, r2, row(6))
        df = dh2.astype(bf)
        dfb[r, :] = df
        vg_o[3:4, :] += colsum(df.astype(f32))
        dx1 = dh2
        for j in range(4):
            cs = slice(j * D, (j + 1) * D)
            dh = (gp[:, cs] * nt(df, w2[cs, :])).astype(bf)
            dhp[r, cs] = dh
            vg_o[8 + j : 9 + j, :] += colsum(dh.astype(f32))
            dx1 = dx1 + nt(dh, wi[:, cs])
        vg_o[4:5, :] += colsum(dx1 * xh1)
        vg_o[5:6, :] += colsum(dx1)
        dh1 = norm_backward(dx1, xh1, r1, row(4))
        dh1_o[r, :] = dh1
        da = dh1.astype(bf)
        dab[r, :] = da
        vg_o[2:3, :] += colsum(da.astype(f32))
        dctx_o[r, :] = nt(da, wo[...]).astype(bf)
        return carry

    lax.fori_loop(0, T // block, one_block, 0)
    outs = []

    def emit(val, dst):
        i = len(outs)
        if i >= 2:
            outs[i - 2].wait()
        stage[i % 2] = val.astype(bf)
        c = pltpu.make_async_copy(stage.at[i % 2], dst, outsem.at[i % 2])
        c.start()
        outs.append(c)

    for j in range(4):
        cs = slice(j * D, (j + 1) * D)
        emit(tn(hb[:, cs], dfb[...]), gw2_h.at[cs, :])
    tr[...] = x1b[...].T
    for j in range(4):
        cs = slice(j * D, (j + 1) * D)
        emit(nn(tr[...], dhp[:, cs]), gwi_h.at[:, cs])
    emit(tn(cb[...], dab[...]), gwo_h)
    outs[7].wait()
    outs[8].wait()


def feed_forward(tok, ctx, cot, vec, wo, wi, w2, block=256):
    return pl.pallas_call(
        functools.partial(ffn_kernel, block),
        in_specs=[VM] * 4 + [ANY] * 3,
        out_specs=[VM] * 4 + [ANY] * 3,
        out_shape=[
            S((T, D), bf), S((T, D), f32), S((T, D), bf), S((16, D), f32), S((D, D), bf), S((D, FF), bf), S((FF, D), bf),
        ],
        scratch_shapes=[
            pltpu.VMEM((D, D), bf), pltpu.VMEM((D, FF), bf), pltpu.VMEM((FF, D), bf), pltpu.VMEM((T, D), bf),
            pltpu.VMEM((T, D), bf), pltpu.VMEM((T, FF), bf), pltpu.VMEM((block, FF), f32), pltpu.VMEM((T, D), bf),
            pltpu.VMEM((T, FF), bf), pltpu.VMEM((T, D), bf), pltpu.VMEM((2, D, D), bf), pltpu.VMEM((D, T), bf),
            pltpu.SemaphoreType.DMA((3,)), pltpu.SemaphoreType.DMA((2,)),
        ],
        compiler_params=pltpu.CompilerParams(vmem_limit_bytes=60 * MIB),
        name="feed_forward",
    )(tok, ctx, cot, vec, wo, wi, w2)


def reduce_kernel(
    gqkv, gwo, gwi, gw2, gvt, s_qkv, s_out, s_in, s_down, s_vec, total,
    acc_a, rs_a, r2_a, r1_a, rz_a, acc_d, rs_d, r2_d, r1_d, rz_d, acc_v, rs_v, r2_v, r1_v, rz_v,
    fin_a, fin_d, rx_a, rx_d, tile, nb1, nb2, gs, gr, ls, xs, xr, ns, nr,
):
    p = Place()
    k = p.k
    far = 1 - k
    enter(p.others + p.zp)
    sent = []

    def go(c):
        c.start()
        sent.append(c)
        return c

    def cols(start, w):
        return pl.ds(pl.multiple_of(start, 128), w)

    items = [(gvt, lambda c: 0, 128, 48, acc_v, rs_v, r2_v, r1_v, rz_v, None)]
    for t in range(3):
        items.append((gw2, lambda c, t=t: c * W3 + t * 128, 128, 192, acc_d.at[t], rs_d.at[t], r2_d.at[t], r1_d.at[t], rz_d.at[t], fin_d.at[t]))
    a = 0
    for t in range(4):
        items.append((gwi, lambda c, t=t: (t + 4 * c) * W3, W3, 48, acc_a.at[a], rs_a.at[a], r2_a.at[a], r1_a.at[a], rz_a.at[a], fin_a.at[a]))
        a += 1
    items.append((gwo, lambda c: c * W3, W3, 48, acc_a.at[a], rs_a.at[a], r2_a.at[a], r1_a.at[a], rz_a.at[a], fin_a.at[a]))
    a += 1
    for t in range(3):
        items.append((gqkv, lambda c, t=t: (t + 3 * c) * W3, W3, 48, acc_a.at[a], rs_a.at[a], r2_a.at[a], r1_a.at[a], rz_a.at[a], fin_a.at[a]))
        a += 1
    n = len(items)

    def add(dst, row0, src, rows):
        step = 96 if rows % 96 == 0 else rows
        def body(i, carry):
            d = pl.ds(pl.multiple_of(row0 + i * step, 16), step)
            s = pl.ds(pl.multiple_of(i * step, 16), step)
            dst[d, :] = (dst[d, :].astype(f32) + src[s, :].astype(f32)).astype(bf)
            return carry
        lax.fori_loop(0, rows // step, body, 0)

    cS, cL, cP, cQ, cZ = {}, {}, {}, {}, {}
    squares = jnp.zeros((8, 128), f32)

    def fold(x):
        rows, width = x.shape
        x = x * x
        tot = jnp.zeros((8, 128), f32)
        for i in range(rows // 8):
            for j in range(width // 128):
                tot = tot + x[i * 8 : (i + 1) * 8, j * 128 : (j + 1) * 128]
        return tot

    for i, (g, col, w, rc, acc, rs, r2, r1, rz, fin) in enumerate(items):
        cL[i] = pltpu.make_async_copy(g.at[:, cols(col(k), w)], acc, ls.at[i])
        cL[i].start()
        cS[i] = go(rcopy(g.at[:, cols(col(far), w)], rs, gs.at[i, 0], gr.at[i, 0], p.sib))
    for s in range(n + 3):
        i = s
        if i < n:
            g, col, w, rc, acc, rs, r2, r1, rz, fin = items[i]
            cL[i].wait()
            cS[i].wait_recv()
            add(acc, 0, rs, 16 * rc)
            grp = lambda dp: pl.ds(pl.multiple_of(dp * 4 * rc, 16), 4 * rc)
            cP[i] = [
                go(rcopy(acc.at[grp(p.dp2), :], r2.at[0], gs.at[i, 1], gr.at[i, 1], p.n2)),
                go(rcopy(acc.at[grp(p.dp3), :], r2.at[1], gs.at[i, 2], gr.at[i, 2], p.n2)),
            ]
        i = s - 1
        if 0 <= i < n:
            g, col, w, rc, acc, rs, r2, r1, rz, fin = items[i]
            cP[i][1].wait_recv()
            add(acc, p.dp1 * 4 * rc, r2.at[1], 4 * rc)
            cQ[i] = go(rcopy(acc.at[pl.ds(pl.multiple_of(p.dp1 * 4 * rc, 16), 4 * rc), :], r1, gs.at[i, 3], gr.at[i, 3], p.n1))
            cP[i][0].wait_recv()
            add(acc, p.dp * 4 * rc, r2.at[0], 4 * rc)
        i = s - 2
        if 0 <= i < n:
            g, col, w, rc, acc, rs, r2, r1, rz, fin = items[i]
            cQ[i].wait_recv()
            add(acc, p.dp * 4 * rc, r1, 4 * rc)
            cZ[i] = []
            for j in range(3):
                there = p.dp * 4 + (p.z + j + 1) % 4
                cZ[i].append(go(rcopy(acc.at[pl.ds(pl.multiple_of(there * rc, 16), rc), :], rz.at[j], gs.at[i, 4 + j], gr.at[i, 4 + j], p.zp[j])))
        i = s - 3
        if 0 <= i < n:
            g, col, w, rc, acc, rs, r2, r1, rz, fin = items[i]
            for c in cZ[i]:
                c.wait_recv()
            own = acc[pl.ds(pl.multiple_of((p.dp * 4 + p.z) * rc, 16), rc), :].astype(f32)
            for j in range(3):
                own = own + rz[j].astype(f32)
            if fin is None:
                mine = jnp.where(k == 0, own[:24], own[24:])
                s_vec[...] = mine
                squares = squares + fold(mine)
            else:
                fin[...] = own
                squares = squares + fold(own)
    cX = []
    for a in range(8):
        cX.append(go(rcopy(fin_a.at[a, pl.ds(pl.multiple_of(far * 24, 8), 24), :], rx_a.at[a], xs.at[a], xr.at[a], p.sib)))
    for t in range(3):
        cX.append(go(rcopy(fin_d.at[t, pl.ds(pl.multiple_of(far * 96, 8), 96), :], rx_d.at[t], xs.at[8 + t], xr.at[8 + t], p.sib)))
    part = jnp.sum(jnp.sum(squares, axis=1, keepdims=True), axis=0, keepdims=True)
    tile[0] = jnp.broadcast_to(part, (8, 128))
    cN = []
    for j in range(3):
        cN.append(go(rcopy(tile.at[0], nb1.at[j], ns.at[j], nr.at[j], p.zp[j])))
    for c in cN:
        c.wait_recv()
    zsum = jnp.zeros((8, 128), f32)
    for zz in range(4):
        val = tile[0]
        for j in range(3):
            val = jnp.where((p.z + 3 - j) % 4 == zz, nb1[j], val)
        zsum = zsum + val
    tile[1] = zsum
    cN = []
    for j in range(7):
        cN.append(go(rcopy(tile.at[1], nb2.at[j], ns.at[3 + j], nr.at[3 + j], p.others[j])))
    keep = lambda c: pl.ds(pl.multiple_of(c * W3, 128), W3)
    my24 = pl.ds(pl.multiple_of(k * 24, 8), 24)
    my96 = pl.ds(pl.multiple_of(k * 96, 8), 96)
    for c in cX:
        c.wait_recv()
    for src, side in ((lambda a: fin_a[a, my24, :], k), (lambda a: rx_a[a], far)):
        for t in range(4):
            s_in[:, cols((t + 4 * side) * W3, W3)] = src(t)
        s_out[:, keep(side)] = src(4)
        for t in range(3):
            val = src(5 + t)
            for j in range(3):
                s_qkv[j, :, cols(side * W3 + t * 128, 128)] = val[:, j * 128 : (j + 1) * 128]
    for t in range(3):
        s_down[:, cols(k * W3 + t * 128, 128)] = fin_d[t, my96, :]
        s_down[:, cols(far * W3 + t * 128, 128)] = rx_d[t]
    for c in cN:
        c.wait_recv()
    msum = jnp.zeros((8, 128), f32)
    for mm in range(8):
        val = tile[1]
        for j in range(7):
            val = jnp.where((p.m + 7 - j) % 8 == mm, nb2[j], val)
        msum = msum + val
    total[...] = msum
    for c in sent:
        c.wait_send()


def reduce_gradients(gqkv, gwo, gwi, gw2, gvt):
    scratch = []
    for count, rows, w in ((8, D, W3), (3, FF, 128), (0, D, 128)):
        lead = (count,) if count else ()
        scratch += [
            pltpu.VMEM(lead + (rows, w), bf), pltpu.VMEM(lead + (rows, w), bf), pltpu.VMEM(lead + (2, rows // 4, w), bf),
            pltpu.VMEM(lead + (rows // 4, w), bf), pltpu.VMEM(lead + (3, rows // 16, w), bf),
        ]
    scratch += [
        pltpu.VMEM((8, 48, W3), f32), pltpu.VMEM((3, 192, 128), f32), pltpu.VMEM((8, 24, W3), f32), pltpu.VMEM((3, 96, 128), f32),
        pltpu.VMEM((2, 8, 128), f32), pltpu.VMEM((3, 8, 128), f32), pltpu.VMEM((7, 8, 128), f32),
        pltpu.SemaphoreType.DMA((12, 7)), pltpu.SemaphoreType.DMA((12, 7)), pltpu.SemaphoreType.DMA((12,)),
        pltpu.SemaphoreType.DMA((11,)), pltpu.SemaphoreType.DMA((11,)), pltpu.SemaphoreType.DMA((10,)), pltpu.SemaphoreType.DMA((10,)),
    ]
    return pl.pallas_call(
        reduce_kernel,
        in_specs=[ANY] * 5,
        out_specs=[VM] * 6,
        out_shape=[
            S((3, 24, D), f32), S((24, D), f32), S((24, FF), f32), S((96, D), f32), S((24, 128), f32), S((8, 128), f32),
        ],
        scratch_shapes=scratch,
        compiler_params=pltpu.CompilerParams(collective_id=1, has_side_effects=True, vmem_limit_bytes=56 * MIB),
        name="reduce_gradients",
    )(gqkv, gwo, gwi, gw2, gvt)


def adam_step(weight, gradient, first_old, second_old, decay_rate, step_rate):
    first_new = moment_decay * first_old + (1.0 - moment_decay) * gradient
    second_new = square_decay * second_old + (1.0 - square_decay) * gradient * gradient
    first_hat = first_new / (1.0 - moment_decay**STEP)
    second_hat = second_new / (1.0 - square_decay**STEP)
    weight_new = weight - step_rate * (first_hat / (jnp.sqrt(second_hat) + adam_epsilon) + decay_rate * weight)
    return (weight_new, first_new, second_new)


def update_kernel(total, *refs):
    w, g, m, u = refs[0:5], refs[5:10], refs[10:15], refs[15:20]
    norm_o, new, first, second = refs[20], refs[21:26], refs[26:31], refs[31:36]
    norm = jnp.sqrt(total[...])
    norm_o[...] = norm
    factor = jnp.minimum(1.0, clip_limit / (norm + 1e-06))[0:1, 0:1]
    for i in range(4):
        n, f, s = adam_step(w[i][...], factor * g[i][...], m[i][...], u[i][...], weight_decay, learn_rate)
        new[i][...] = n
        first[i][...] = f
        second[i][...] = s
    wide = jnp.concatenate([g[4][...], jnp.zeros((104, 128), f32)], axis=0).T[:12, :24]
    n, f, s = adam_step(w[4][...], factor * wide, m[4][...], u[4][...], 0.0, vector_rate)
    new[4][...] = n
    first[4][...] = f
    second[4][...] = s


def update(total, weights, grads, firsts, seconds):
    shapes = [S(w.shape, f32) for w in weights]
    return pl.pallas_call(
        update_kernel,
        in_specs=[VM] * 21,
        out_specs=[VM] * 16,
        out_shape=[S((8, 128), f32)] + shapes * 3,
        compiler_params=pltpu.CompilerParams(vmem_limit_bytes=40 * MIB),
        name="clip_and_update",
    )(total, *weights, *grads, *firsts, *seconds)


def segment_ids(lengths):
    bounds = jnp.cumsum(lengths, axis=-1)
    places = jnp.arange(T, dtype=jnp.int32)
    return jnp.sum((places[:, None] >= bounds[None, :]).astype(jnp.int32), axis=-1)


def pairs_last(a):
    return a.reshape(3, D, PAIRS, 128).transpose(1, 2, 0, 3).reshape(D, 3 * D)


def per_device(
    small, tokens, cotangent, lengths, qkv_weight, out_weight, in_weight, down_weight, vectors,
    qkv_first, out_first, in_first, down_first, vec_first, qkv_second, out_second, in_second, down_second, vec_second,
):
    weights = (qkv_weight, out_weight, in_weight, down_weight, vectors)
    firsts = (qkv_first, out_first, in_first, down_first, vec_first)
    seconds = (qkv_second, out_second, in_second, down_second, vec_second)
    axes = ("dp", "fsdp")
    if small:
        wqkv, wo, wi, w2, vt = gather_weights(*weights)
        vec = vt[:, :16].astype(f32).T
    else:
        gather = lambda a, axis: lax.all_gather(a.astype(bf), axes, axis=axis, tiled=True)
        wqkv = pairs_last(gather(qkv_weight, 1))
        wo, wi, w2 = gather(out_weight, 0), gather(in_weight, 0), gather(down_weight, 0)
        vec = jnp.concatenate([gather(vectors, 1).astype(f32), jnp.zeros((4, D), f32)], axis=0)
    bias = jnp.stack([vec[0], jnp.zeros_like(vec[0]), vec[1]]).reshape(3, PAIRS, 128).transpose(1, 0, 2).reshape(1, 3 * D)
    seg = segment_ids(lengths[0])
    lane = jnp.arange(128)
    match = seg[:, None] == lane[None, :]
    onehot = match.astype(bf)
    neg = jnp.where(match | (lane >= lengths.shape[1])[None, :], 0.0, -1e30).astype(bf)
    q, k, v, ctx, lse = attend(tokens, wqkv, bias, onehot, neg)
    result, dh1, dctx, vg, gwo, gwi, gw2 = feed_forward(tokens, ctx, cotangent, vec, wo, wi, w2)
    gqkv, input_grad, vg_qv = attend_back(tokens, wqkv, dh1, q, k, v, dctx, ctx, lse, onehot, neg)
    vg = vg + vg_qv
    if small:
        gvt = jnp.concatenate([vg.T.astype(bf), jnp.zeros((D, 112), bf)], axis=1)
        *grads, total = reduce_gradients(gqkv, gwo, gwi, gw2, gvt)
        updated = update(total, weights, grads, firsts, seconds)
        return (result, input_grad, updated[0][0, 0], *updated[1:])
    scatter = lambda a, axis: lax.psum_scatter(a.astype(f32), axes, scatter_dimension=axis, tiled=True)
    gqkv = gqkv.reshape(D, PAIRS, 3, 128).transpose(2, 0, 1, 3).reshape(3, D, D)
    grads = (scatter(gqkv, 1), scatter(gwo, 0), scatter(gwi, 0), scatter(gw2, 0), scatter(vg[:12], 1))
    grad_norm = jnp.sqrt(lax.psum(sum(jnp.sum(g * g) for g in grads), axes))
    factor = jnp.minimum(1.0, clip_limit / (grad_norm + 1e-06))
    updated = []
    for i in range(5):
        rates = (0.0, vector_rate) if i == 4 else (weight_decay, learn_rate)
        updated.append(adam_step(weights[i], factor * grads[i], firsts[i], seconds[i], *rates))
    return (result, input_grad, grad_norm, *[u[j] for j in range(3) for u in updated])


def solution(mesh):
    rows = P(("dp", "fsdp"), None)
    deep = P(None, ("dp", "fsdp"), None)
    wide = P(None, ("dp", "fsdp"))
    group = (deep, rows, rows, rows, wide)
    small = mesh.shape["dp"] == 4 and mesh.shape["fsdp"] == 8
    return jax.shard_map(
        functools.partial(per_device, small),
        mesh=mesh,
        in_specs=(rows, rows, rows) + group * 3,
        out_specs=(rows, rows, P()) + group * 3,
        check_vma=False,
    )
```

time: 1080 us -> 333 us (0.31)
  waiting for transfers between devices: 463 us -> 0 us
  Pallas kernels: 0 us -> 306 us
  matrix products: 300 us -> 0 us
  blocking collectives: 125 us -> 0 us
  other arithmetic: 111 us -> 1.54 us
  local copies, waits for them, and re-layouts: 43.8 us -> 19.3 us
  between operations: 20.2 us -> 1.3 us
    pallas_call x0 -> x6, Pallas kernels: none -> 306 us  [the longest x1 84.7 us: reduce_gradients(): pl.pallas_call(reduce_kernel, in_specs=[ANY] * 5, out_specs=[VM] * 6, out...]
    dot_general x32 -> x0, matrix products: 300 us -> none  [the longest x4 44.3 us: masked_scores(): jnp.einsum('qhd,khd->hqk', query_block, key_heads, preferred_element_type...]
    reduce_scatter x3 -> x0, waiting for transfers between devices: 278 us -> none  [the longest x1 139 us: per_device(): lax.psum_scatter(grad_down, ('dp', 'fsdp'), scatter_dimension=0, tiled=True)]
    unnamed x9 -> x0, waiting for transfers between devices: 116 us -> none
    all_gather x4 -> x0, waiting for transfers between devices: 70 us -> none  [the longest x1 31.5 us: per_device(): lax.all_gather(in_weight.astype(jnp.bfloat16), ('dp', 'fsdp'), axis=0, ti...]
    convert_element_type x7 -> x3, other arithmetic: 51.9 us -> 1.21 us  [the longest x1 0.81 us: per_device(): gvt = jnp.concatenate([vg.T.astype(bf), jnp.zeros((D, 112), bf)], axis=1)]
    reduce_sum x16 -> x1, other arithmetic: 44.4 us -> 0.09 us  [segment_ids(): jnp.sum((places[:, None] >= bounds[None, :]).astype(jnp.int32), axis=-1)]
    all_gather x1 -> x0, blocking collectives: 44 us -> none  [per_device(): lax.all_gather(vectors.astype(jnp.bfloat16), ('dp', 'fsdp'), axis=1, tile...]
  transfers between devices with their start and end apart: 8 -> 0, of which waited for: 6 -> 0; matrix products, arithmetic and copies ran while one was open for 34% -> 0% of each run, Pallas kernels for 0% -> 0%
where the time goes in v1:
time: 333 us; the launch traced here: 328 us
  Pallas kernels  306 us (92%)
  local copies, waits for them, and re-layouts  19.3 us (6%)
    pallas_call x1, Pallas kernels, reduce_gradients(): pl.pallas_call(reduce_kernel, in_specs=[ANY] * 5, out_specs=[VM] * 6, out...  84.7 us
    pallas_call x1, Pallas kernels, gather_weights(): pl.pallas_call(gather_kernel, in_specs=[VM] * 5, out_specs=[ANY] * 5, out...  76.3 us
    pallas_call x1, Pallas kernels, feed_forward(): pl.pallas_call(functools.partial(ffn_kernel, block), in_specs=[VM] * 4 +...  62.7 us
    pallas_call x1, Pallas kernels, attend_back(): pl.pallas_call(functools.partial(backward_kernel, block), grid=(PAIRS,),...  52.8 us
    pallas_call x1, Pallas kernels, attend(): pl.pallas_call(functools.partial(forward_kernel, block), grid=(PAIRS,), i...  27.1 us
    unnamed x70, local copies, waits for them, and re-layouts  16.9 us

profile of v1, /device:TPU:0, one launch (start us, length us, event | category | flops | bytes accessed | tf_op | source)
XLA Modules:
  0.0 327.8 jit_solution(768376907604239992)
XLA Ops:
  0.7 0.1 pad.2.clone
  0.7 0.7 copy.53
  1.5 0.1 reduce
  1.6 0.1 convert_reduce_fusion
  1.7 0.2 select_convert_fusion.neg
  1.9 0.0 copy-start.2
  1.9 0.2 fusion.1.onehot
  2.1 0.0 copy-start.7
  2.2 1.0 copy-done.7
  3.1 1.0 copy-done.9
  4.1 0.9 copy-done.11
  5.0 0.9 copy-done.13
  5.9 0.7 copy-done.27
  6.6 76.3 %gather_weights.1 = (bf16[768,2304]{1,0:T(8,128)(2,1)S(1)}, bf16[768,768]{1,0:T(8,128)(2,1)S(1)}, bf16[768,3072]{1,0:T(8,128)(2,1)S(1)}, bf16[3072,768]{1,0:T(8,128)(2,1)}, bf16[768,128]{1,0:T(8,128)(2,1)S(1)}) custom-call(f32[3,24,768]{2,1,0:T(8,128)S(1)} %copy-done.11, f32[24,768]{1,0:T(8,128)S(1)} %copy-done.13, f32[24,3072]{1,0:T(8,128)S(1)} %copy-done.7, ...), custom_call_target="tpu_custom_call" | custom-call | tf_op jit(solution)/shard_map/gather_weights/pallas_call | solution.py:201
  82.9 1.8 copy-done
  84.7 2.1 copy-done.1
  86.8 1.0 copy-done.6
  87.9 0.1 copy.51
  88.0 0.0 copy-start.33
  88.0 0.1 pad_maximum_fusion
  88.2 27.1 %attend.1 = (bf16[1024,768]{1,0:T(8,128)(2,1)S(1)}, bf16[1024,768]{1,0:T(8,128)(2,1)S(1)}, bf16[1024,768]{1,0:T(8,128)(2,1)}, f32[1024,768]{1,0:T(8,128)}, f32[6,1024,128]{2,1,0:T(8,128)}) custom-call(bf16[1024,768]{1,0:T(8,128)(2,1)} %tok.5, bf16[768,2304]{1,0:T(8,128)(2,1)} %copy-done, f32[1,2304]{1,0:T(1,128)S(1)} %reshape.72.bias, ...), custom_call_target="tpu_custom_call" | custom-call | tf_op jit(solution)/shard_map/attend/pallas_call | solution.py:257
  115.3 1.1 copy-done.4
  116.4 1.2 copy-done.5
  117.6 62.7 %feed_forward.1 = (bf16[1024,768]{1,0:T(8,128)(2,1)}, f32[1024,768]{1,0:T(8,128)}, bf16[1024,768]{1,0:T(8,128)(2,1)}, f32[16,768]{1,0:T(8,128)}, bf16[768,768]{1...) custom-call(bf16[1024,768]{1,0:T(8,128)(2,1)} %tok.5, f32[1024,768]{1,0:T(8,128)} %get-tuple-element.62.ctx.ctx_i, ...), custom_call_target="tpu_custom_call" | custom-call | tf_op jit(solution)/shard_map/feed_forward/pallas_call | solution.py:470
  180.3 0.0 copy-start.34
  180.3 52.8 %attend_back.1 = (bf16[768,2304]{1,0:T(8,128)(2,1)}, bf16[1024,768]{1,0:T(8,128)(2,1)}, f32[16,768]{1,0:T(8,128)}) custom-call(bf16[1024,768]{1,0:T(8,128)(2,1)} %tok.5, bf16[768,2304]{1,0:T(8,128)(2,1)} %copy-done, f32[1024,768]{1,0:T(8,128)} %get-tuple-element.67.dh1, bf16[1024,768]{1,0:T(8,128)(2,1)} %copy-done.4, bf16[1024,768]{1,0:T(8,128)(2,1)} %copy-done.5, ...), custom_call_target="tpu_custom_call" | custom-call | tf_op jit(solution)/shard_map/attend_back/pallas_call | solution.py:347
  233.1 0.8 add_convert_fusion
  234.0 0.2 copy.54
  234.1 0.7 concatenate.3.gvt
  234.9 0.0 copy-start.15
  234.9 0.0 copy-start.16
  234.9 0.0 copy-start.17
  234.9 0.0 copy-start.18
  234.9 0.0 copy-start.21
  234.9 0.0 copy-start.22
  234.9 0.0 copy-start.24
  234.9 0.0 copy-start.25
  235.0 0.0 copy-start.28
  235.0 0.0 copy-start.30
  235.0 84.7 %reduce_gradients.1 = (f32[3,24,768]{2,1,0:T(8,128)}, f32[24,768]{1,0:T(8,128)}, f32[24,3072]{1,0:T(8,128)}, f32[96,768]{1,0:T(8,128)}, f32[24,128]{1,0:T(8,128)}, /*index=5*/f32[8,128]{1,0:T(8,128)}) custom-call(bf16[768,2304]{1,0:T(8,128)(2,1)} %get-tuple-element.74.gqkv, bf16[768,768]{1,0:T(8,128)(2,1)} %get-tuple-element.75.gwo, ...), custom_call_target="tpu_custom_call" | custom-call | tf_op jit(solution)/shard_map/reduce_gradients/pallas_call | solution.py:655
  319.8 1.0 copy-done.19
  320.8 1.0 copy-done.20
  321.8 0.9 copy-done.23
  322.7 0.9 copy-done.26
  323.6 0.7 copy-done.29
  324.3 0.7 copy-done.32
  325.0 2.1 clip_and_update.1
  327.1 0.5 slice.15
  (47 shorter events, 0.2 us)
Async XLA Ops:
  1.9 113.4 %copy-start.2 = (bf16[1024,128]{1,0:T(8,128)(2,1)}, bf16[1024,128]{1,0:T(8,128)(2,1)S(1)}, u32[]{:S(2)}) copy-start(bf16[1024,128]{1,0:T(8,128)(2,1)S(1)} %select_convert_fusion.neg) | copy-start | bytes 786436
  2.1 1.0 copy-start.7
  3.1 1.0 copy-start.9
  4.1 0.9 copy-start.11
  5.0 0.9 copy-start.13
  5.9 0.7 copy-start.27
  6.6 108.7 %copy-start.3 = (bf16[1024,128]{1,0:T(8,128)(2,1)}, bf16[1024,128]{1,0:T(8,128)(2,1)S(1)}, u32[]{:S(2)}) copy-start(bf16[1024,128]{1,0:T(8,128)(2,1)S(1)} %fusion.1.onehot) | copy-start | bytes 786436
  82.9 1.8 copy-start
  84.7 2.1 copy-start.1
  86.8 1.0 copy-start.6
  88.0 27.3 %copy-start.33 = (f32[16,768]{1,0:T(8,128)}, f32[16,768]{1,0:T(8,128)S(1)}, u32[]{:S(2)}) copy-start(f32[16,768]{1,0:T(8,128)S(1)} %convert_bitcast_fusion.vec) | copy-start | bytes 147460
  115.3 1.1 copy-start.4
  116.4 1.2 copy-start.5
  180.3 52.8 %copy-start.34 = (f32[16,768]{1,0:T(8,128)S(1)}, f32[16,768]{1,0:T(8,128)}, u32[]{:S(2)}) copy-start(f32[16,768]{1,0:T(8,128)} %get-tuple-element.78) | copy-start | bytes 147460
  234.8 84.8 %copy-start.8 = (f32[24,3072]{1,0:T(8,128)S(1)}, f32[24,3072]{1,0:T(8,128)}, u32[]{:S(2)}) copy-start(f32[24,3072]{1,0:T(8,128)} %refs_2_.1) | copy-start | bytes 884740
  234.8 84.8 %copy-start.10 = (f32[96,768]{1,0:T(8,128)S(1)}, f32[96,768]{1,0:T(8,128)}, u32[]{:S(2)}) copy-start(f32[96,768]{1,0:T(8,128)} %refs_3_.1) | copy-start | bytes 884740
  234.8 84.9 %copy-start.12 = (f32[3,24,768]{2,1,0:T(8,128)S(1)}, f32[3,24,768]{2,1,0:T(8,128)}, u32[]{:S(2)}) copy-start(f32[3,24,768]{2,1,0:T(8,128)} %refs_0_.1) | copy-start | bytes 663556
  234.9 84.9 %copy-start.14 = (f32[24,768]{1,0:T(8,128)S(1)}, f32[24,768]{1,0:T(8,128)}, u32[]{:S(2)}) copy-start(f32[24,768]{1,0:T(8,128)} %refs_1_.1) | copy-start | bytes 221188
  234.9 84.9 %copy-start.15 = (f32[24,3072]{1,0:T(8,128)S(1)}, f32[24,3072]{1,0:T(8,128)}, u32[]{:S(2)}) copy-start(f32[24,3072]{1,0:T(8,128)} %refs_12_.1) | copy-start | bytes 884740
  234.9 84.9 %copy-start.16 = (f32[96,768]{1,0:T(8,128)S(1)}, f32[96,768]{1,0:T(8,128)}, u32[]{:S(2)}) copy-start(f32[96,768]{1,0:T(8,128)} %refs_13_.1) | copy-start | bytes 884740
  234.9 84.9 %copy-start.17 = (f32[24,3072]{1,0:T(8,128)S(1)}, f32[24,3072]{1,0:T(8,128)}, u32[]{:S(2)}) copy-start(f32[24,3072]{1,0:T(8,128)} %refs_17_.1) | copy-start | bytes 884740
  234.9 84.9 %copy-start.18 = (f32[96,768]{1,0:T(8,128)S(1)}, f32[96,768]{1,0:T(8,128)}, u32[]{:S(2)}) copy-start(f32[96,768]{1,0:T(8,128)} %refs_18_.1) | copy-start | bytes 884740
  234.9 84.9 %copy-start.21 = (f32[3,24,768]{2,1,0:T(8,128)S(1)}, f32[3,24,768]{2,1,0:T(8,128)}, u32[]{:S(2)}) copy-start(f32[3,24,768]{2,1,0:T(8,128)} %refs_10_.1) | copy-start | bytes 663556
  234.9 84.9 %copy-start.22 = (f32[3,24,768]{2,1,0:T(8,128)S(1)}, f32[3,24,768]{2,1,0:T(8,128)}, u32[]{:S(2)}) copy-start(f32[3,24,768]{2,1,0:T(8,128)} %refs_15_.1) | copy-start | bytes 663556
  234.9 84.9 %copy-start.24 = (f32[24,768]{1,0:T(8,128)S(1)}, f32[24,768]{1,0:T(8,128)}, u32[]{:S(2)}) copy-start(f32[24,768]{1,0:T(8,128)} %refs_11_.1) | copy-start | bytes 221188
  234.9 84.9 %copy-start.25 = (f32[24,768]{1,0:T(8,128)S(1)}, f32[24,768]{1,0:T(8,128)}, u32[]{:S(2)}) copy-start(f32[24,768]{1,0:T(8,128)} %refs_16_.1) | copy-start | bytes 221188
  235.0 84.9 %copy-start.28 = (f32[12,24]{1,0:T(8,128)S(1)}, f32[12,24]{1,0:T(8,128)}, u32[]{:S(2)}) copy-start(f32[12,24]{1,0:T(8,128)} %refs_4_.1) | copy-start | bytes 3460
  235.0 84.9 %copy-start.30 = (f32[12,24]{1,0:T(8,128)S(1)}, f32[12,24]{1,0:T(8,128)}, u32[]{:S(2)}) copy-start(f32[12,24]{1,0:T(8,128)} %refs_14_.1) | copy-start | bytes 3460
  235.0 84.8 %copy-start.31 = (f32[12,24]{1,0:T(8,128)S(1)}, f32[12,24]{1,0:T(8,128)}, u32[]{:S(2)}) copy-start(f32[12,24]{1,0:T(8,128)} %refs_19_.1) | copy-start | bytes 3460
  319.8 1.0 copy-start.19
  320.8 1.0 copy-start.20
  321.8 0.9 copy-start.23
  322.7 0.9 copy-start.26
  323.6 0.7 copy-start.29
  324.3 0.7 copy-start.32
